TPU v7x, 128 devices: a whole 4x4x4 slice. The times are simulated.
128 devices in a mesh: seq: 16 (over z_hi, y, core), tp: 8 (over z_lo, x).
Axes of the slice: x: 4, y: 4, z: 4 (z_hi: 2, z_lo: 2; z = z_hi * 2 + z_lo), core: 2. Of those that a mesh axis runs over, the one named last changes fastest.
Arguments:
- inputs: bfloat16 [2048, 4096], P('seq', 'tp'), may hold values from -6 to 6
- target: bfloat16 [2048, 4096], P('seq', 'tp'), may hold values from -6 to 6
- feature_slots: int32 [2048, 16, 8], P(None, 'seq'), may hold values from -1 to 4095, as said below
- w_enc: bfloat16 [65536, 4096], P('seq', 'tp'), may hold values from -0.09375 to 0.09375
- b_enc: float32 [65536], P('seq'), may hold values from -1 to 1
- w_dec: bfloat16 [65536, 4096], P('seq', 'tp'), may hold values from -0.75 to 0.75
- b_dec: float32 [4096], P('tp'), may hold values from -3 to 3
- w_skip: bfloat16 [4096, 4096], P('seq', 'tp'), may hold values from -0.09375 to 0.09375
Outputs:
- reconstruction: bfloat16 [2048, 4096], P('seq', 'tp')
- grad_enc: bfloat16 [65536, 4096], P('seq', 'tp')
- grad_dec: bfloat16 [65536, 4096], P('seq', 'tp')
- grad_benc: float32 [65536], P('seq')
- grad_bdec: float32 [4096], P('tp')
- grad_skip: bfloat16 [4096, 4096], P('seq', 'tp')
Inputs may be any that keep to these rules, and one draw needn't show every extreme that they name: feature_slots[t, o, j] is a feature number inside block o of 4096 features, or -1 for an empty slot; each token has exactly 64 live slots naming distinct features, at most 8 in one block, and every token fills all 8 slots of at least one block.
All inputs are finite; a program needn't handle non-finite values.
Results may differ from a plain program's by a relative error of at most 0.0059.
Values may be sent and summed in bfloat16 or wider, within the bound.
A program may use at most 128 MiB of HBM per device.

v0:
```python
import math

import jax
import jax.numpy as jnp
from jax import lax
from jax.sharding import PartitionSpec as P


def shards(inputs, target, feature_slots, w_enc, b_enc, w_dec, b_dec, w_skip):
    local_ids = feature_slots[:, 0, :]
    live_float = (local_ids >= 0).astype(jnp.float32)
    index_table = jnp.maximum(local_ids, 0)
    all_tokens = lax.all_gather(inputs, "seq", axis=0, tiled=True)
    total_rows = all_tokens.shape[0]
    block_rows = min(512, total_rows)
    block_count = total_rows // block_rows
    block_feats = w_enc.shape[0]

    def encode_block(position):
        first_row = position * block_rows
        tok_rows = lax.dynamic_slice_in_dim(all_tokens, first_row, block_rows, 0)
        id_rows = lax.dynamic_slice_in_dim(index_table, first_row, block_rows, 0)
        return jnp.einsum(
            "bd,bsd->bs", tok_rows, w_enc[id_rows], preferred_element_type=jnp.float32
        )

    partial_pre = lax.map(encode_block, jnp.arange(block_count)).reshape(total_rows, -1)
    summed_pre = lax.psum(partial_pre, "tp")
    preact = summed_pre + b_enc[index_table]
    active = (jnp.maximum(preact, 0.0) * live_float).astype(jnp.bfloat16)
    row_count = inputs.shape[0] * lax.axis_size("seq")
    sub_rows = math.gcd(row_count, 512)

    def decode_block(position):
        first_row = position * sub_rows
        id_rows = lax.dynamic_slice_in_dim(index_table, first_row, sub_rows, 0)
        act_rows = lax.dynamic_slice_in_dim(active, first_row, sub_rows, 0)
        partial_value = jnp.einsum(
            "bs,bsd->bd", act_rows, w_dec[id_rows], preferred_element_type=jnp.float32
        )
        return partial_value

    decoded = lax.psum_scatter(
        lax.map(decode_block, jnp.arange(row_count // sub_rows)).reshape(row_count, -1),
        "seq",
        scatter_dimension=0,
        tiled=True,
    )
    row_features = lax.all_gather(inputs, "tp", axis=1, tiled=True)
    columns = row_features
    skip_out = jnp.dot(
        columns,
        lax.all_gather(w_skip, "seq", axis=0, tiled=True),
        preferred_element_type=jnp.float32,
    )
    predicted = decoded + skip_out + b_dec
    reconstruction = predicted.astype(jnp.bfloat16)
    residual = (predicted - target.astype(jnp.float32)).astype(jnp.bfloat16)
    all_resid = lax.all_gather(residual, "seq", axis=0, tiled=True)

    def back_block(position):
        first_row = position * block_rows
        res_rows = lax.dynamic_slice_in_dim(all_resid, first_row, block_rows, 0)
        id_rows = lax.dynamic_slice_in_dim(index_table, first_row, block_rows, 0)
        return jnp.einsum(
            "bd,bsd->bs", res_rows, w_dec[id_rows], preferred_element_type=jnp.float32
        )

    partial_back = lax.map(back_block, jnp.arange(block_count)).reshape(total_rows, -1)
    summed_back = lax.psum(partial_back, "tp")
    slope = summed_back * (preact > 0.0).astype(jnp.float32) * live_float
    grad_benc = (
        jnp.zeros(b_enc.shape, jnp.float32).at[index_table.reshape(-1)].add(slope.reshape(-1))
    )
    slope_half = slope.astype(jnp.bfloat16)
    row_numbers = jnp.arange(block_rows, dtype=jnp.int32)[:, None]
    contract_rows = (((0,), (0,)), ((), ()))

    def grad_block(carry, position):
        enc_total, dec_total = carry
        first_row = position * block_rows
        tok_rows = lax.dynamic_slice_in_dim(all_tokens, first_row, block_rows, 0)
        res_rows = lax.dynamic_slice_in_dim(all_resid, first_row, block_rows, 0)
        id_rows = lax.dynamic_slice_in_dim(index_table, first_row, block_rows, 0)
        slope_rows = lax.dynamic_slice_in_dim(slope_half, first_row, block_rows, 0)
        act_rows = lax.dynamic_slice_in_dim(active, first_row, block_rows, 0)
        empty_table = jnp.zeros((block_rows, block_feats), jnp.bfloat16)
        slope_table = empty_table.at[row_numbers, id_rows].add(slope_rows)
        act_table = empty_table.at[row_numbers, id_rows].add(act_rows)
        enc_total = enc_total + lax.dot_general(
            slope_table, tok_rows, contract_rows, preferred_element_type=jnp.float32
        )
        dec_total = dec_total + lax.dot_general(
            act_table, res_rows, contract_rows, preferred_element_type=jnp.float32
        )
        return ((enc_total, dec_total), position)

    zero_grads = jnp.zeros(w_enc.shape, jnp.float32)
    totals = lax.scan(grad_block, (zero_grads, zero_grads), jnp.arange(block_count))[0]
    grad_bdec = jnp.sum(all_resid.astype(jnp.float32), axis=0)
    columns = row_features
    grad_skip = lax.psum_scatter(
        jnp.dot(columns.T, residual, preferred_element_type=jnp.float32),
        "seq",
        scatter_dimension=0,
        tiled=True,
    ).astype(jnp.bfloat16)
    return (
        reconstruction,
        totals[0].astype(jnp.bfloat16),
        totals[1].astype(jnp.bfloat16),
        grad_benc,
        grad_bdec,
        grad_skip,
    )


def solution(mesh):
    in_specs = (
        P("seq", "tp"),
        P("seq", "tp"),
        P(None, "seq", None),
        P("seq", "tp"),
        P("seq"),
        P("seq", "tp"),
        P("tp"),
        P("seq", "tp"),
    )
    out_specs = (P("seq", "tp"), P("seq", "tp"), P("seq", "tp"), P("seq"), P("tp"), P("seq", "tp"))
    return jax.shard_map(shards, mesh=mesh, in_specs=in_specs, out_specs=out_specs, check_vma=False)
```

profile of v0, /device:TPU:0, one launch (start us, length us, event | category | flops | bytes accessed | tf_op | source)
XLA Modules:
  0.0 1195.6 jit_solution(16714371156747533695)
XLA Ops:
  9.3 52.1 %all-gather.5.cloned.1.call-done = bf16[2048,512]{1,0:T(8,128)(2,1)} async-done(((bf16[128,512]{1,0:T(8,128)(2,1)}), bf16[2048,512]{1,0:T(8,128)(2,1)}) %all-gather.5.cloned.1.call-update) | async-done | bytes 2097168 | tf_op jit(solution)/shard_map/all_gather | solution.py:13
  61.4 107.5 %while.43 = (s32[]{:T(128)}, f32[4,512,8]{1,2,0:T(8,128)S(1)}, s32[4]{0:T(128)S(1)}, bf16[2048,512]{1,0:T(8,128)(2,1)}, s32[2048,8]{1,0:T(8,128)S(1)}, /*index=5...) while((s32[]{:T(128)}, f32[4,512,8]{1,2,0:T(8,128)S(1)}, s32[4]{0:T(128)S(1)}, ...), condition=%wide.region_1.2_spmd, body=%wide.region_0.1_spmd.sunk | while | flops 4210694 | bytes 14352563 | solution.py:27
  64.0 20.2 %gather_fusion = bf16[4096,512]{1,0:T(8,128)(2,1)} fusion(bf16[4096,512]{1,0:T(8,128)(2,1)} %get-tuple-element.500, s32[4096]{0:T(1024)S(1)} %broadcast_clamp_fusion.7), kind=kCustom, calls=%fused_computation.clone.1 | custom fusion | bytes 8404992 | tf_op jit(solution)/shard_map/while/body/eval_jaxpr/gather | solution.py:24
  90.9 20.2 %gather_fusion = bf16[4096,512]{1,0:T(8,128)(2,1)} fusion(bf16[4096,512]{1,0:T(8,128)(2,1)} %get-tuple-element.500, s32[4096]{0:T(1024)S(1)} %broadcast_clamp_fusion.7), kind=kCustom, calls=%fused_computation.clone.1 | custom fusion | bytes 8404992 | tf_op jit(solution)/shard_map/while/body/eval_jaxpr/gather | solution.py:24
  117.7 20.2 %gather_fusion = bf16[4096,512]{1,0:T(8,128)(2,1)} fusion(bf16[4096,512]{1,0:T(8,128)(2,1)} %get-tuple-element.500, s32[4096]{0:T(1024)S(1)} %broadcast_clamp_fusion.7), kind=kCustom, calls=%fused_computation.clone.1 | custom fusion | bytes 8404992 | tf_op jit(solution)/shard_map/while/body/eval_jaxpr/gather | solution.py:24
  172.8 90.5 %gather_fusion.3 = f32[16384]{0:T(1024)S(1)} fusion(f32[4096]{0:T(1024)S(1)} %copy-done, s32[16384]{0:T(1024)S(1)} %broadcast_clamp_fusion.3), kind=kCustom, calls=%fused_computation.3 | custom fusion | bytes 196608 | tf_op jit(solution)/shard_map/gather | solution.py:29
  268.0 105.3 %while.44 = (s32[]{:T(128)}, f32[4,512,512]{2,1,0:T(8,128)}, s32[4]{0:T(128)S(1)}, bf16[2048,8]{0,1:T(8,128)(2,1)S(1)}, s32[2048,8]{1,0:T(8,128)S(1)}, /*index=5...) while((s32[]{:T(128)}, f32[4,512,512]{2,1,0:T(8,128)}, s32[4]{0:T(128)S(1)}, ...), condition=%wide.region_4.5_spmd, body=%wide.region_3.4_spmd.sunk | while | flops 4210694 | bytes 15884467 | solution.py:44
  269.6 20.2 %gather_fusion.1 = bf16[4096,512]{1,0:T(8,128)(2,1)} fusion(bf16[4096,512]{1,0:T(8,128)(2,1)} %get-tuple-element.530, s32[4096]{0:T(1024)S(1)} %broadcast_clamp_fusion.8), kind=kCustom, calls=%fused_computation.1.clone.1 | custom fusion | bytes 8404992 | tf_op jit(solution)/shard_map/while/body/eval_jaxpr/gather | solution.py:39
  295.9 20.3 %gather_fusion.1 = bf16[4096,512]{1,0:T(8,128)(2,1)} fusion(bf16[4096,512]{1,0:T(8,128)(2,1)} %get-tuple-element.530, s32[4096]{0:T(1024)S(1)} %broadcast_clamp_fusion.8), kind=kCustom, calls=%fused_computation.1.clone.1 | custom fusion | bytes 8404992 | tf_op jit(solution)/shard_map/while/body/eval_jaxpr/gather | solution.py:39
  373.4 79.1 %reduce-scatter.3.cloned.1.call-done = f32[128,512]{1,0:T(8,128)} async-done(((f32[2048,512]{1,0:T(8,128)}), f32[128,512]{1,0:T(8,128)}) %reduce-scatter.3.cloned.1.call-update) | async-done | bytes 262160 | tf_op jit(solution)/shard_map/reduce_scatter | solution.py:43
  456.5 47.0 %all-gather.11.cloned.1.call-done = bf16[2048,512]{1,0:T(8,128)(2,1)} async-done(((bf16[128,512]{1,0:T(8,128)(2,1)}), bf16[2048,512]{1,0:T(8,128)(2,1)}) %all-gather.11.cloned.1.call-update) | async-done | bytes 2097168 | tf_op jit(solution)/shard_map/all_gather | solution.py:59
  503.5 107.5 %while.45 = (s32[]{:T(128)}, f32[4,512,8]{1,2,0:T(8,128)S(1)}, s32[4]{0:T(128)S(1)}, bf16[2048,512]{1,0:T(8,128)(2,1)}, s32[2048,8]{1,0:T(8,128)S(1)}, /*index=5...) while((s32[]{:T(128)}, f32[4,512,8]{1,2,0:T(8,128)S(1)}, s32[4]{0:T(128)S(1)}, ...), condition=%wide.region_7.8_spmd, body=%wide.region_6.7_spmd.sunk | while | flops 4210694 | bytes 14352563 | solution.py:69
  506.1 20.2 %gather_fusion.2 = bf16[4096,512]{1,0:T(8,128)(2,1)} fusion(bf16[4096,512]{1,0:T(8,128)(2,1)} %get-tuple-element.560, s32[4096]{0:T(1024)S(1)} %broadcast_clamp_fusion.9), kind=kCustom, calls=%fused_computation.2.clone.1 | custom fusion | bytes 8404992 | tf_op jit(solution)/shard_map/while/body/eval_jaxpr/gather | solution.py:66
  619.6 68.6 %all-reduce.5.cloned.1.call-done = f32[2048,8]{1,0:T(8,128)} async-done(((f32[2048,8]{1,0:T(8,128)}), f32[2048,8]{1,0:T(8,128)}) %all-reduce.5.cloned.1.call-update) | async-done | bytes 65552 | tf_op jit(solution)/shard_map/psum | solution.py:70
  691.6 395.8 %while.46 = (s32[]{:T(128)}, f32[4096,512]{1,0:T(8,128)}, f32[4096,512]{1,0:T(8,128)}, s32[4]{0:T(128)S(1)}, s32[2048,8]{0,1:T(8,128)S(1)}, /*index=5*/bf16[2048...) while((s32[]{:T(128)}, f32[4096,512]{1,0:T(8,128)}, ...), condition=%wide.region_12.13_spmd.clone, body=%wide.region_9.12_spmd.clone.sunk | while | flops 4303437824 | bytes 85238048 | solution.py:99
  694.7 31.5 %scatter_custom_fusion.15 = bf16[2097152]{0:T(1024)(128)(2,1)} fusion(s32[4096]{0:T(1024)S(1)} %reshape.207, bf16[4096]{0:T(1024)(128)(2,1)S(1)} %reshape.210, bf16[]{:T(256)} %constant.47.clone.2..sunk), kind=kCustom, calls=%fused_computation.30.clone.1 | custom fusion | flops 4096 | bytes 4194306 | tf_op jit(solution)/shard_map/while
  733.6 31.5 %scatter_custom_fusion.14 = bf16[2097152]{0:T(1024)(128)(2,1)} fusion(s32[4096]{0:T(1024)S(1)} %reshape.207, bf16[4096]{0:T(1024)(128)(2,1)S(1)} %reshape.208, bf16[]{:T(256)} %constant.47.clone.2..sunk), kind=kCustom, calls=%fused_computation.32.clone.1 | custom fusion | flops 4096 | bytes 4194306 | tf_op jit(solution)/shard_map/while
  789.3 31.5 %scatter_custom_fusion.15 = bf16[2097152]{0:T(1024)(128)(2,1)} fusion(s32[4096]{0:T(1024)S(1)} %reshape.207, bf16[4096]{0:T(1024)(128)(2,1)S(1)} %reshape.210, bf16[]{:T(256)} %constant.47.clone.2..sunk), kind=kCustom, calls=%fused_computation.30.clone.1 | custom fusion | flops 4096 | bytes 4194306 | tf_op jit(solution)/shard_map/while
  828.1 31.5 %scatter_custom_fusion.14 = bf16[2097152]{0:T(1024)(128)(2,1)} fusion(s32[4096]{0:T(1024)S(1)} %reshape.207, bf16[4096]{0:T(1024)(128)(2,1)S(1)} %reshape.208, bf16[]{:T(256)} %constant.47.clone.2..sunk), kind=kCustom, calls=%fused_computation.32.clone.1 | custom fusion | flops 4096 | bytes 4194306 | tf_op jit(solution)/shard_map/while
  889.7 31.5 %scatter_custom_fusion.15 = bf16[2097152]{0:T(1024)(128)(2,1)} fusion(s32[4096]{0:T(1024)S(1)} %reshape.207, bf16[4096]{0:T(1024)(128)(2,1)S(1)} %reshape.210, bf16[]{:T(256)} %constant.47.clone.2..sunk), kind=kCustom, calls=%fused_computation.30.clone.1 | custom fusion | flops 4096 | bytes 4194306 | tf_op jit(solution)/shard_map/while
  928.5 31.5 %scatter_custom_fusion.14 = bf16[2097152]{0:T(1024)(128)(2,1)} fusion(s32[4096]{0:T(1024)S(1)} %reshape.207, bf16[4096]{0:T(1024)(128)(2,1)S(1)} %reshape.208, bf16[]{:T(256)} %constant.47.clone.2..sunk), kind=kCustom, calls=%fused_computation.32.clone.1 | custom fusion | flops 4096 | bytes 4194306 | tf_op jit(solution)/shard_map/while
  990.1 31.5 %scatter_custom_fusion.15 = bf16[2097152]{0:T(1024)(128)(2,1)} fusion(s32[4096]{0:T(1024)S(1)} %reshape.207, bf16[4096]{0:T(1024)(128)(2,1)S(1)} %reshape.210, bf16[]{:T(256)} %constant.47.clone.2..sunk), kind=kCustom, calls=%fused_computation.30.clone.1 | custom fusion | flops 4096 | bytes 4194306 | tf_op jit(solution)/shard_map/while
  1028.9 31.5 %scatter_custom_fusion.14 = bf16[2097152]{0:T(1024)(128)(2,1)} fusion(s32[4096]{0:T(1024)S(1)} %reshape.207, bf16[4096]{0:T(1024)(128)(2,1)S(1)} %reshape.208, bf16[]{:T(256)} %constant.47.clone.2..sunk), kind=kCustom, calls=%fused_computation.32.clone.1 | custom fusion | flops 4096 | bytes 4194306 | tf_op jit(solution)/shard_map/while
  1097.3 89.5 %scatter_custom_fusion.2 = f32[4096]{0:T(1024)} fusion(s32[16384]{0:T(1024)} %copy-done.12, f32[16384]{0:T(1024)S(1)} %reshape.141, f32[]{:T(128)} %constant.62.clone.1), kind=kCustom, calls=%fused_computation.56 | custom fusion | flops 16384 | bytes 16896 | tf_op jit(solution)/shard_map/scatter-add | solution.py:73
  (250 shorter events, 370.2 us)
Async XLA Ops:
  7.2 165.6 %copy-start = (f32[4096]{0:T(1024)S(1)}, f32[4096]{0:T(1024)}, u32[]{:S(2)}) copy-start(f32[4096]{0:T(1024)} %param.20) | copy-start | bytes 49156
  7.2 54.2 %all-gather.5.cloned.1.call-start = ((), (), s32[]{:S(2)}) async-start(), calls=%async_computation.2 | async-start | bytes 2228224 | tf_op jit(solution)/shard_map/all_gather | solution.py:13
  7.9 256.1 %all-reduce.3.cloned.1.call-start = ((), (), s32[]{:S(2)}) async-start(), calls=%async_computation.3 | async-start | bytes 2097152 | tf_op jit(solution)/shard_map/psum | solution.py:28
  9.1 52.3 %copy-start.8 = (s32[2048,1,8]{2,0,1:T(8,128)}, s32[2048,1,8]{2,0,1:T(8,128)S(1)}, u32[]{:S(2)}) copy-start(s32[2048,1,8]{2,0,1:T(8,128)S(1)} %copy.23) | copy-start | bytes 196612
  168.9 94.4 %copy-start.4 = (s32[2048,8]{1,0:T(8,128)}, s32[2048,8]{1,0:T(8,128)S(1)}, u32[]{:S(2)}) copy-start(s32[2048,8]{1,0:T(8,128)S(1)} %get-tuple-element.622) | copy-start | bytes 196612
  170.3 203.1 %all-gather.7.cloned.1.call-start = ((), (), s32[]{:S(2)}) async-start(), calls=%async_computation.5 | async-start | bytes 1179648 | tf_op jit(solution)/shard_map/all_gather | solution.py:49
  171.0 202.3 %all-gather.9.cloned.1.call-start = ((), (), s32[]{:S(2)}) async-start(), calls=%async_computation.6 | async-start | bytes 4456448 | tf_op jit(solution)/shard_map/all_gather | solution.py:53
  171.6 280.9 %reduce-scatter.3.cloned.1.call-start = ((), (), s32[]{:S(2)}) async-start(), calls=%async_computation.4 | async-start | bytes 4456448 | tf_op jit(solution)/shard_map/reduce_scatter | solution.py:43
  172.8 91.2 %copy-start.9 = (s32[2048,1,8]{2,0,1:T(8,128)S(1)}, s32[2048,1,8]{2,0,1:T(8,128)}, u32[]{:S(2)}) copy-start(s32[2048,1,8]{2,0,1:T(8,128)} %copy-done.8) | copy-start | bytes 196612
  373.2 79.2 %copy-start.13 = (bf16[128,512]{1,0:T(8,128)(2,1)S(1)}, bf16[128,512]{1,0:T(8,128)(2,1)}, u32[]{:S(2)}) copy-start(bf16[128,512]{1,0:T(8,128)(2,1)} %param.17) | copy-start | bytes 393220
  373.3 79.2 %copy-start.16 = (f32[512]{0:T(512)S(1)}, f32[512]{0:T(512)}, u32[]{:S(2)}) copy-start(f32[512]{0:T(512)} %param.22) | copy-start | bytes 6148
  373.3 130.2 %all-gather.11.cloned.1.call-start = ((), (), s32[]{:S(2)}) async-start(), calls=%async_computation.7 | async-start | bytes 2228224 | tf_op jit(solution)/shard_map/all_gather | solution.py:59
  456.5 231.8 %all-reduce.5.cloned.1.call-start = ((), (), s32[]{:S(2)}) async-start(), calls=%async_computation.8 | async-start | bytes 2097152 | tf_op jit(solution)/shard_map/psum | solution.py:70
  503.5 109.1 %copy-start.10 = (bf16[128,4096]{1,0:T(8,128)(2,1)S(1)}, bf16[128,4096]{1,0:T(8,128)(2,1)}, u32[]{:S(2)}) copy-start(bf16[128,4096]{1,0:T(8,128)(2,1)} %all-gather.7.cloned.1.call-done) | copy-start | bytes 3145732
  503.5 109.1 %copy-start.11 = (bf16[128,512]{1,0:T(8,128)(2,1)S(1)}, bf16[128,512]{1,0:T(8,128)(2,1)}, u32[]{:S(2)}) copy-start(bf16[128,512]{1,0:T(8,128)(2,1)} %get-tuple-element.302) | copy-start | bytes 393220
  612.4 574.4 %reduce-scatter.5.cloned.1.call-start = ((), (), s32[]{:S(2)}) async-start(), calls=%async_computation.9 | async-start | bytes 8912896 | tf_op jit(solution)/shard_map/reduce_scatter | solution.py:102
  617.4 74.2 %copy-start.14 = (s32[2]{0:T(128)S(1)}, s32[2]{0:T(128)}, u32[]{:S(2)}) copy-start(s32[2]{0:T(128)} %constant.145) | copy-start | bytes 28
  617.4 74.2 %copy-start.15 = (s32[2]{0:T(128)S(1)}, s32[2]{0:T(128)}, u32[]{:S(2)}) copy-start(s32[2]{0:T(128)} %constant.144) | copy-start | bytes 28
  772.4 8.1 copy-start.2
  866.9 10.6 copy-start.2
  967.3 10.6 copy-start.2
  1067.7 10.6 copy-start.2
  1087.4 7.3 copy-start.3
  1093.7 95.0 %copy-start.1 = (f32[4096]{0:T(1024)S(1)}, f32[4096]{0:T(1024)}, u32[]{:S(2)}) copy-start(f32[4096]{0:T(1024)} %param.20) | copy-start | bytes 49156
  (4 other events, 10.2 us)
Sparse Core Ops, SparseCore 0:
  10.5 50.9 all-gather.4
  170.4 75.7 all-reduce.2
  247.8 38.5 all-gather.6
  288.7 55.4 all-gather.8
  373.4 79.0 reduce-scatter.2
  456.6 46.8 all-gather.10
  612.5 75.7 all-reduce.4
  693.2 102.1 reduce-scatter.4
where the time goes:
time: 1200 us
  local copies, waits for them, and re-layouts  434 us (36%)
  other arithmetic  359 us (30%)
  waiting for transfers between devices  249 us (21%)
  matrix products  128 us (11%)
  between operations  14.4 us (1%)
    while x20, other arithmetic  253 us
    gather x2, local copies, waits for them, and re-layouts, shards(): preact = summed_pre + b_enc[index_table]  91.1 us
    scatter-add x1, other arithmetic, shards(): jnp.zeros(b_enc.shape, jnp.float32).at[index_table.reshape(-1)]  89.5 us
    gather x4, local copies, waits for them, and re-layouts, decode_block(): w_dec[id_rows]  80.9 us
    gather x4, local copies, waits for them, and re-layouts, back_block(): w_dec[id_rows]  80.7 us
    gather x4, local copies, waits for them, and re-layouts, encode_block(): w_enc[id_rows]  80.7 us
    reduce_scatter x1, waiting for transfers between devices, shards(): lax.psum_scatter(lax.map(decode_block, jnp.arange(row_count // sub_rows))...  79.1 us
    psum x1, waiting for transfers between devices, shards(): summed_back = lax.psum(partial_back, 'tp')  68.6 us
  transfers between devices with their start and end apart: 8, of which 4 were waited for; matrix products, arithmetic and copies ran while one was open for 59% of the time, Pallas kernels for 0%

commit v1 on v0

v1 whole, which is shorter than its diff:
```python
import functools

import jax
import jax.numpy as jnp
from jax import lax
from jax.experimental import pallas as pl
from jax.experimental.pallas import tpu as pltpu
from jax.sharding import PartitionSpec as P

MESH = pl.DeviceIdType.MESH
BF16 = jnp.bfloat16
F32 = jnp.float32
VMEM_LIMIT = 56 << 20

N_SEQ = 16
N_TP = 8
ROWS = 128
TOKENS = 2048
COLS = 512
FEATS = 4096
SKIP = 256
SLOTS = 8


class Place:
    def __init__(self):
        self.s = lax.axis_index("seq")
        self.p = lax.axis_index("tp")
        s, p = self.s, self.p
        self.c = lax.rem(s, 2)
        self.y = lax.rem(lax.div(s, 2), 4)
        self.zh = lax.div(s, 8)
        self.x = lax.rem(p, 4)
        self.zl = lax.div(p, 4)
        self.mate = (s + 1 - 2 * self.c, p)
        self.up = (self.seq(0, 1), p)
        self.down = (self.seq(0, 3), p)
        self.far = (self.seq(1, 0), p)
        self.right = (s, self.tp(0, 1))
        self.left = (s, self.tp(0, 3))
        self.side = (s, self.tp(1, 0))

    def seq(self, b, dy, other_core=False):
        zh = 1 - self.zh if b else self.zh
        c = 1 - self.c if other_core else self.c
        return (zh * 4 + lax.rem(self.y + dy, 4)) * 2 + c

    def tp(self, b, dx):
        zl = 1 - self.zl if b else self.zl
        return zl * 4 + lax.rem(self.x + dx, 4)


def greet(devices):
    barrier = pltpu.get_barrier_semaphore()
    for dev in devices:
        pl.semaphore_signal(barrier, inc=1, device_id=dev, device_id_type=MESH)
    pl.semaphore_wait(barrier, len(devices))


class Sender:
    def __init__(self, send, recv, here):
        self.send, self.recv, self.here = send, recv, here
        self.started = []

    def start(self, i, src, dst, dev):
        copy = pltpu.make_async_remote_copy(
            src_ref=src, dst_ref=dst, send_sem=self.send.at[i], recv_sem=self.recv.at[i],
            device_id=dev, device_id_type=MESH,
        )
        copy.start()
        self.started.append(copy)

    def wait(self, i, dst):
        pltpu.make_async_remote_copy(
            src_ref=dst, dst_ref=dst, send_sem=self.send.at[i], recv_sem=self.recv.at[i],
            device_id=self.here, device_id_type=MESH,
        ).wait_recv()

    def drain(self):
        for copy in self.started:
            copy.wait_send()
        self.started = []


SEQ_KINDS = 19


def seq_rows(q, half=None):
    if half is None:
        return pl.ds(pl.multiple_of(q * ROWS, ROWS), ROWS)
    return pl.ds(pl.multiple_of(q * ROWS + half * (ROWS // 2), ROWS // 2), ROWS // 2)


def gather_seq(at, net, own, out):
    def blk(b, dy, half=None, other=False):
        return out.at[seq_rows(at.seq(b, dy, other), half)]

    mine = out.at[seq_rows(at.s)]
    net.start(8, own, mine, at.far)
    net.start(0, own, mine, at.up)
    net.start(1, own, mine, at.down)
    net.start(9, own, mine, at.mate)
    yield
    for b in (0, 1):
        k, m = 4 * b, 9 + 5 * b
        if b:
            net.wait(8, blk(1, 0))
            net.start(4, blk(1, 0), blk(1, 0), at.up)
            net.start(5, blk(1, 0), blk(1, 0), at.down)
            net.start(m, blk(1, 0), blk(1, 0), at.mate)
        net.wait(k, blk(b, 3))
        net.start(k + 2, blk(b, 3, 0), blk(b, 3, 0), at.up)
        net.start(m + 1, blk(b, 3), blk(b, 3), at.mate)
        net.wait(k + 1, blk(b, 1))
        net.start(k + 3, blk(b, 1, 1), blk(b, 1, 1), at.down)
        net.start(m + 2, blk(b, 1), blk(b, 1), at.mate)
        yield
    for b in (0, 1):
        k, m = 4 * b, 9 + 5 * b
        net.wait(k + 2, blk(b, 2, 0))
        net.start(m + 3, blk(b, 2, 0), blk(b, 2, 0), at.mate)
        net.wait(k + 3, blk(b, 2, 1))
        net.start(m + 4, blk(b, 2, 1), blk(b, 2, 1), at.mate)
    yield
    for b in (0, 1):
        m = 9 + 5 * b
        net.wait(m, blk(b, 0, None, True))
        net.wait(m + 1, blk(b, 3, None, True))
        net.wait(m + 2, blk(b, 1, None, True))
        net.wait(m + 3, blk(b, 2, 0, True))
        net.wait(m + 4, blk(b, 2, 1, True))
    yield


def gather_kernel(x_ref, all_ref, skip_ref, send, recv, send2, recv2, local):
    at = Place()
    here = (at.s, at.p)
    half_p = lax.div(at.s, 2)
    stay = half_p == at.p
    around = [at.mate, at.up, at.down, at.far, at.right, at.left, at.side]
    barrier = pltpu.get_barrier_semaphore()
    for dev in around:
        pl.semaphore_signal(barrier, inc=1, device_id=dev, device_id_type=MESH)

    same, cross = (2 * at.p + at.c, half_p), (2 * at.p + 1 - at.c, half_p)
    pl.semaphore_signal(barrier, inc=1, device_id=cross, device_id_type=MESH)

    @pl.when(jnp.logical_not(stay))
    def _():
        pl.semaphore_signal(barrier, inc=1, device_id=same, device_id_type=MESH)

    pl.semaphore_wait(barrier, len(around) + 2 - stay.astype(jnp.int32))

    keep = pltpu.make_async_copy(x_ref, all_ref.at[seq_rows(at.s)], local.at[0])
    keep.start()
    net = Sender(send, recv, here)
    net2 = Sender(send2, recv2, here)
    steps = gather_seq(at, net, x_ref, all_ref)
    next(steps)

    def part(h):
        return x_ref.at[:, pl.ds(pl.multiple_of(h * SKIP, SKIP), SKIP)]

    land = skip_ref.at[seq_rows(at.s)]
    net2.start(1, part(1 - at.c), land, cross)
    from_same = skip_ref.at[seq_rows(2 * at.p + at.c)]
    from_cross = skip_ref.at[seq_rows(2 * at.p + 1 - at.c)]

    @pl.when(jnp.logical_not(stay))
    def _():
        copy = pltpu.make_async_remote_copy(
            src_ref=part(at.c), dst_ref=land, send_sem=send2.at[0], recv_sem=recv2.at[0],
            device_id=same, device_id_type=MESH,
        )
        copy.start()
        copy.wait_send()
        net2.wait(0, from_same)

    @pl.when(stay)
    def _():
        copy = pltpu.make_async_copy(part(at.c), land, local.at[1])
        copy.start()
        copy.wait()

    net2.wait(1, from_cross)

    def piece(b, dx, half=None):
        q = at.tp(b, dx)
        if half is None:
            return skip_ref.at[pl.ds(pl.multiple_of(q * 256, 256), 256)]
        return skip_ref.at[pl.ds(pl.multiple_of(q * 256 + half * 128, 128), 128)]

    net2.start(10, piece(0, 0), piece(0, 0), at.side)
    net2.start(2, piece(0, 0), piece(0, 0), at.right)
    net2.start(3, piece(0, 0), piece(0, 0), at.left)
    next(steps)
    net2.wait(10, piece(1, 0))
    net2.start(6, piece(1, 0), piece(1, 0), at.right)
    net2.start(7, piece(1, 0), piece(1, 0), at.left)
    next(steps)
    for b in (0, 1):
        k = 2 + 4 * b
        net2.wait(k, piece(b, 3))
        net2.start(k + 2, piece(b, 3, 0), piece(b, 3, 0), at.right)
        net2.wait(k + 1, piece(b, 1))
        net2.start(k + 3, piece(b, 1, 1), piece(b, 1, 1), at.left)
    next(steps)
    for b in (0, 1):
        k = 2 + 4 * b
        net2.wait(k + 2, piece(b, 2, 0))
        net2.wait(k + 3, piece(b, 2, 1))
    next(steps)
    keep.wait()
    net.drain()
    net2.drain()


def gather(x):
    return pl.pallas_call(
        gather_kernel,
        out_shape=[
            jax.ShapeDtypeStruct((TOKENS, COLS), BF16),
            jax.ShapeDtypeStruct((TOKENS, SKIP), BF16),
        ],
        in_specs=[pl.BlockSpec(memory_space=pl.ANY)],
        out_specs=[pl.BlockSpec(memory_space=pl.ANY)] * 2,
        scratch_shapes=[
            pltpu.SemaphoreType.DMA((SEQ_KINDS,)),
            pltpu.SemaphoreType.DMA((SEQ_KINDS,)),
            pltpu.SemaphoreType.DMA((11,)),
            pltpu.SemaphoreType.DMA((11,)),
            pltpu.SemaphoreType.DMA((2,)),
        ],
        compiler_params=pltpu.CompilerParams(
            collective_id=0, has_side_effects=True, vmem_limit_bytes=VMEM_LIMIT
        ),
        name="gather_inputs",
    )(x)


def pick_kernel(with_bias, x_ref, id_ref, w_ref, *rest):
    b_ref, o_ref = rest if with_bias else (None, rest[0])
    ids = id_ref[...]
    low = ids & 127
    high = ids >> 7
    width = 1024
    acc = jnp.zeros(ids.shape, F32)
    for c in range(FEATS // width):
        cols = slice(c * width, (c + 1) * width)
        dots = lax.dot_general(
            x_ref[...], w_ref[cols, :], (((1,), (1,)), ((), ())), preferred_element_type=F32
        )
        if with_bias:
            dots = dots + b_ref[:, cols]
        for g in range(width // 128):
            got = jnp.take_along_axis(
                dots[:, g * 128 : (g + 1) * 128], low, axis=1, mode="promise_in_bounds"
            )
            acc = jnp.where(high == c * (width // 128) + g, got, acc)
    for r in range(ids.shape[0] // 128):
        turned = acc[r * 128 : (r + 1) * 128, :].T
        o_ref[:, r * 128 : (r + 1) * 128] = turned[:SLOTS, :]


def pick(name, x, ids, w, bias=None, rows=256):
    specs = [
        pl.BlockSpec((rows, COLS), lambda i: (i, 0)),
        pl.BlockSpec((rows, 128), lambda i: (i, 0)),
        pl.BlockSpec((FEATS, COLS), lambda i: (0, 0)),
    ]
    args = [x, ids, w]
    if bias is not None:
        specs.append(pl.BlockSpec((1, FEATS), lambda i: (0, 0)))
        args.append(bias)
    return pl.pallas_call(
        functools.partial(pick_kernel, bias is not None),
        grid=(TOKENS // rows,),
        in_specs=specs,
        out_specs=pl.BlockSpec((SLOTS, rows), lambda i: (0, i)),
        out_shape=jax.ShapeDtypeStruct((SLOTS, TOKENS), F32),
        compiler_params=pltpu.CompilerParams(vmem_limit_bytes=VMEM_LIMIT),
        name=name,
    )(*args)


def sum_kernel(x_ref, o_ref, parts, send, recv, send2, recv2):
    at = Place()
    width = TOKENS // N_TP
    here = (at.s, at.p)
    peers = [(at.s, lax.rem(at.p + d, N_TP)) for d in range(1, N_TP)]
    greet(peers)

    def lanes(q):
        return pl.ds(pl.multiple_of(q * width, width), width)

    net = Sender(send, recv, here)
    for d in range(1, N_TP):
        net.start(d, x_ref.at[:, lanes(peers[d - 1][1])], parts.at[d], peers[d - 1])
    total = x_ref[:, lanes(at.p)]
    for d in range(1, N_TP):
        net.wait(d, parts.at[d])
        total = total + parts[d]
    o_ref[:, lanes(at.p)] = total
    net2 = Sender(send2, recv2, here)
    for d in range(1, N_TP):
        net2.start(d, o_ref.at[:, lanes(at.p)], o_ref.at[:, lanes(at.p)], peers[d - 1])
    for d in range(1, N_TP):
        net2.wait(d, o_ref.at[:, lanes(lax.rem(at.p + N_TP - d, N_TP))])
    net.drain()
    net2.drain()


def sum_tp(x, number, name):
    return pl.pallas_call(
        sum_kernel,
        out_shape=jax.ShapeDtypeStruct((SLOTS, TOKENS), F32),
        in_specs=[pl.BlockSpec(memory_space=pltpu.VMEM)],
        out_specs=pl.BlockSpec(memory_space=pltpu.VMEM),
        scratch_shapes=[pltpu.VMEM((N_TP, SLOTS, TOKENS // N_TP), F32)]
        + [pltpu.SemaphoreType.DMA((N_TP,))] * 4,
        compiler_params=pltpu.CompilerParams(
            collective_id=number, has_side_effects=True, vmem_limit_bytes=VMEM_LIMIT
        ),
        name=name,
    )(x)


def decode_kernel(key_ref, pre_ref, base_ref, w_ref, xs_ref, ws_ref, o_ref, a_ref):
    rows = key_ref.shape[0]
    filler = jnp.zeros((128 - SLOTS, 128), F32)
    for t in range(rows // 128):
        act = jnp.maximum(pre_ref[:, t * 128 : (t + 1) * 128], 0.0)
        act = jnp.concatenate([act, filler], axis=0).T
        for r in range(8):
            line = slice(t * 128 + r * 16, t * 128 + (r + 1) * 16)
            key = key_ref[line, :]
            val = act[r * 16 : (r + 1) * 16, :]
            keys, vals = [], []
            for j in range(SLOTS):
                keys.append(jnp.broadcast_to(key[:, j : j + 1], (16, 128)).astype(BF16))
                vals.append(jnp.broadcast_to(val[:, j : j + 1], (16, 128)).astype(BF16))
            for g in range(FEATS // 128):
                base = base_ref[:, g * 128 : (g + 1) * 128]
                acc = jnp.zeros((16, 128), BF16)
                for j in range(SLOTS):
                    acc = jnp.where(keys[j] == base, vals[j], acc)
                a_ref[line, g * 128 : (g + 1) * 128] = acc
    o_ref[...] = jnp.dot(a_ref[...], w_ref[...], preferred_element_type=F32) + jnp.dot(
        xs_ref[...], ws_ref[...], preferred_element_type=F32
    )


def decode(key, pre, base, w, xs, ws, rows=256):
    return pl.pallas_call(
        decode_kernel,
        grid=(TOKENS // rows,),
        in_specs=[
            pl.BlockSpec((rows, SLOTS), lambda i: (i, 0)),
            pl.BlockSpec((SLOTS, rows), lambda i: (0, i)),
            pl.BlockSpec((16, FEATS), lambda i: (0, 0)),
            pl.BlockSpec((FEATS, COLS), lambda i: (0, 0)),
            pl.BlockSpec((rows, SKIP), lambda i: (i, 0)),
            pl.BlockSpec((SKIP, COLS), lambda i: (0, 0)),
        ],
        out_specs=pl.BlockSpec((rows, COLS), lambda i: (i, 0)),
        out_shape=jax.ShapeDtypeStruct((TOKENS, COLS), F32),
        scratch_shapes=[pltpu.VMEM((rows, FEATS), BF16)],
        compiler_params=pltpu.CompilerParams(vmem_limit_bytes=VMEM_LIMIT),
        name="decode",
    )(key, pre, base, w, xs, ws)


def residual_kernel(
    part, target, bias, recon, all_ref, mrecv, out_buf, half_in, full_in, far_out, far_in, res,
    msend, mrcv, ysend, yrcv, send, recv, local,
):
    at = Place()
    here = (at.s, at.p)
    greet([at.mate, at.up, at.down, at.far])
    mnet = Sender(msend, mrcv, here)
    ynet = Sender(ysend, yrcv, here)
    order = [(b, dy) for b in (1, 0) for dy in (2, 1, 3, 0)]
    for k, (b, dy) in enumerate(order):
        mnet.start(k, part.at[seq_rows(at.seq(b, dy, True))], mrecv.at[k], at.mate)
    H = ROWS // 2

    def pair(k, half=None):
        b, dy = order[k]
        rows = seq_rows(at.seq(b, dy), half)
        mine = slice(0, ROWS) if half is None else slice(half * H, (half + 1) * H)
        return part[rows, :] + mrecv[k, mine, :]

    for i, b in enumerate((1, 0)):
        k = 4 * i
        mnet.wait(k, mrecv.at[k])
        out_buf[3 * i] = pair(k).astype(BF16)
        ynet.start(4 * i, out_buf.at[3 * i, pl.ds(0, H)], half_in.at[2 * i], at.up)
        ynet.start(4 * i + 1, out_buf.at[3 * i, pl.ds(H, H)], half_in.at[2 * i + 1], at.down)
    for i, b in enumerate((1, 0)):
        k = 4 * i
        mnet.wait(k + 1, mrecv.at[k + 1])
        out_buf[3 * i + 1, H:, :] = pair(k + 1, 1).astype(BF16)
        ynet.wait(4 * i, half_in.at[2 * i])
        out_buf[3 * i + 1, :H, :] = (pair(k + 1, 0) + half_in[2 * i].astype(F32)).astype(BF16)
        ynet.start(4 * i + 2, out_buf.at[3 * i + 1], full_in.at[2 * i], at.up)
        mnet.wait(k + 2, mrecv.at[k + 2])
        out_buf[3 * i + 2, :H, :] = pair(k + 2, 0).astype(BF16)
        ynet.wait(4 * i + 1, half_in.at[2 * i + 1])
        out_buf[3 * i + 2, H:, :] = (pair(k + 2, 1) + half_in[2 * i + 1].astype(F32)).astype(BF16)
        ynet.start(4 * i + 3, out_buf.at[3 * i + 2], full_in.at[2 * i + 1], at.down)
    mnet.wait(3, mrecv.at[3])
    total = pair(3)
    ynet.wait(2, full_in.at[0])
    ynet.wait(3, full_in.at[1])
    far_out[...] = total + full_in[0].astype(F32) + full_in[1].astype(F32)
    ynet.start(8, far_out, far_in, at.far)
    mnet.wait(7, mrecv.at[7])
    total = pair(7)
    ynet.wait(6, full_in.at[2])
    ynet.wait(7, full_in.at[3])
    total = total + full_in[2].astype(F32) + full_in[3].astype(F32) + bias[...]
    ynet.wait(8, far_in)
    total = total + far_in[...]
    recon[...] = total.astype(BF16)
    res[...] = (total - target[...].astype(F32)).astype(BF16)
    keep = pltpu.make_async_copy(res, all_ref.at[seq_rows(at.s)], local.at[0])
    keep.start()
    net = Sender(send, recv, here)
    for _ in gather_seq(at, net, res, all_ref):
        pass
    keep.wait()
    mnet.drain()
    ynet.drain()
    net.drain()


def residuals(part, target, bias):
    vm = pl.BlockSpec(memory_space=pltpu.VMEM)
    dma = pltpu.SemaphoreType.DMA
    return pl.pallas_call(
        residual_kernel,
        out_shape=[
            jax.ShapeDtypeStruct((ROWS, COLS), BF16),
            jax.ShapeDtypeStruct((TOKENS, COLS), BF16),
        ],
        in_specs=[vm, vm, vm],
        out_specs=[vm, pl.BlockSpec(memory_space=pl.ANY)],
        scratch_shapes=[
            pltpu.VMEM((8, ROWS, COLS), F32),
            pltpu.VMEM((6, ROWS, COLS), BF16),
            pltpu.VMEM((4, ROWS // 2, COLS), BF16),
            pltpu.VMEM((4, ROWS, COLS), BF16),
            pltpu.VMEM((ROWS, COLS), F32),
            pltpu.VMEM((ROWS, COLS), F32),
            pltpu.VMEM((ROWS, COLS), BF16),
            dma((8,)), dma((8,)), dma((9,)), dma((9,)),
            dma((SEQ_KINDS,)), dma((SEQ_KINDS,)), dma((1,)),
        ],
        compiler_params=pltpu.CompilerParams(
            collective_id=2, has_side_effects=True, vmem_limit_bytes=VMEM_LIMIT
        ),
        name="residuals",
    )(part, target, bias)


def grad_kernel(
    key_ref, pre_ref, back_ref, base_ref, x_ref, r_ref, ge_ref, gd_ref, st_ref, at_ref
):
    feats = base_ref.shape[0]
    for t in range(TOKENS // 128):
        lanes = slice(t * 128, (t + 1) * 128)
        pre = pre_ref[:, lanes]
        slope = jnp.where(pre > 0.0, back_ref[:, lanes], 0.0)
        act = jnp.maximum(pre, 0.0)
        key = key_ref[:, lanes]
        keys, slopes, acts = [], [], []
        for j in range(SLOTS):
            row = slice(j, j + 1)
            keys.append(jnp.broadcast_to(key[row, :], (16, 128)).astype(BF16))
            slopes.append(jnp.broadcast_to(slope[row, :], (16, 128)).astype(BF16))
            acts.append(jnp.broadcast_to(act[row, :], (16, 128)).astype(BF16))
        for r in range(feats // 16):
            lines = slice(r * 16, (r + 1) * 16)
            base = base_ref[lines, :]
            s_acc = jnp.zeros((16, 128), BF16)
            a_acc = jnp.zeros((16, 128), BF16)
            for j in range(SLOTS):
                hit = keys[j] == base
                s_acc = jnp.where(hit, slopes[j], s_acc)
                a_acc = jnp.where(hit, acts[j], a_acc)
            st_ref[lines, lanes] = s_acc
            at_ref[lines, lanes] = a_acc
    ge_ref[...] = jnp.dot(st_ref[...], x_ref[...], preferred_element_type=F32).astype(BF16)
    gd_ref[...] = jnp.dot(at_ref[...], r_ref[...], preferred_element_type=F32).astype(BF16)


def grads(key, pre, back, base, x, r, feats=512):
    slots = pl.BlockSpec((SLOTS, TOKENS), lambda i: (0, 0))
    whole = pl.BlockSpec((TOKENS, COLS), lambda i: (0, 0))
    out = pl.BlockSpec((feats, COLS), lambda i: (i, 0))
    return pl.pallas_call(
        grad_kernel,
        grid=(FEATS // feats,),
        in_specs=[slots, slots, slots, pl.BlockSpec((feats, 128), lambda i: (i, 0)), whole, whole],
        out_specs=[out, out],
        out_shape=[jax.ShapeDtypeStruct((FEATS, COLS), BF16)] * 2,
        scratch_shapes=[pltpu.VMEM((feats, TOKENS), BF16)] * 2,
        compiler_params=pltpu.CompilerParams(vmem_limit_bytes=VMEM_LIMIT),
        name="grads",
    )(key, pre, back, base, x, r)


def small_kernel(id_ref, pre_ref, back_ref, xs_ref, r_ref, gb_ref, gs_ref, bd_ref):
    total = jnp.zeros((FEATS // 128, 128), F32)
    contract = (((0,), (0,)), ((), ()))
    pairs = (((1,), (1,)), ((), ()))
    for t in range(TOKENS // 512):
        lanes = slice(t * 512, (t + 1) * 512)
        ids = id_ref[:, lanes]
        high, low = ids >> 7, ids & 127
        slope = jnp.where(pre_ref[:, lanes] > 0.0, back_ref[:, lanes], 0.0)
        top = slope.astype(BF16).astype(F32)
        rest = slope - top
        rest_top = rest.astype(BF16).astype(F32)
        last = rest - rest_top
        lines = lax.broadcasted_iota(jnp.int32, (FEATS // 128, 512), 0)
        lanes128 = lax.broadcasted_iota(jnp.int32, (128, 512), 0)
        for j in range(SLOTS):
            row = slice(j, j + 1)
            one = jnp.where(high[row, :] == lines, 1.0, 0.0).astype(BF16)
            hit = low[row, :] == lanes128
            for value in (top, rest_top, last):
                table = jnp.where(hit, value[row, :], 0.0).astype(BF16)
                total += lax.dot_general(one, table, pairs, preferred_element_type=F32)
    gb_ref[...] = total
    gs_ref[...] = lax.dot_general(
        xs_ref[...], r_ref[...], contract, preferred_element_type=F32
    ).astype(BF16)
    bd_ref[...] = jnp.dot(jnp.ones((8, TOKENS), BF16), r_ref[...], preferred_element_type=F32)


def small_grads(ids, pre, back, xs, r):
    return pl.pallas_call(
        small_kernel,
        in_specs=[pl.BlockSpec(memory_space=pltpu.VMEM)] * 5,
        out_specs=[pl.BlockSpec(memory_space=pltpu.VMEM)] * 3,
        out_shape=[
            jax.ShapeDtypeStruct((FEATS // 128, 128), F32),
            jax.ShapeDtypeStruct((SKIP, COLS), BF16),
            jax.ShapeDtypeStruct((8, COLS), F32),
        ],
        compiler_params=pltpu.CompilerParams(vmem_limit_bytes=VMEM_LIMIT),
        name="small_grads",
    )(ids, pre, back, xs, r)


def shards(inputs, target, feature_slots, w_enc, b_enc, w_dec, b_dec, w_skip):
    ids = feature_slots[:, 0, :]
    ids_t = ids.T
    tiled = jnp.tile(jnp.maximum(ids, 0), (1, 128 // SLOTS))

    def key_of(number):
        high = jnp.left_shift(jnp.uint32(1), (number >> 7).astype(jnp.uint32)).astype(F32)
        return (128 + (number & 127)).astype(F32) * high

    key = jnp.where(ids >= 0, key_of(jnp.maximum(ids, 0)), -1.0)
    key_t = jnp.where(ids_t >= 0, key_of(jnp.maximum(ids_t, 0)), -1.0)
    base = key_of(jnp.arange(FEATS, dtype=jnp.int32)).astype(BF16)
    base_row = jnp.broadcast_to(base[None, :], (16, FEATS))
    base_col = jnp.broadcast_to(base[:, None], (FEATS, 128))
    bias = jnp.where(lax.axis_index("tp") == 0, b_enc, 0.0)[None, :]

    all_x, x_skip = gather(inputs)
    pre = sum_tp(pick("encode", all_x, tiled, w_enc, bias), 1, "sum_pre")
    part = decode(key, pre, base_row, w_dec, x_skip, w_skip)
    recon, all_r = residuals(part, target, b_dec[None, :])
    back = sum_tp(pick("backward", all_r, tiled, w_dec), 1, "sum_back")
    grad_enc, grad_dec = grads(key_t, pre, back, base_col, all_x, all_r)
    grad_benc, grad_skip, grad_bdec = small_grads(ids_t, pre, back, x_skip, all_r)
    return recon, grad_enc, grad_dec, grad_benc.reshape(-1), grad_bdec[0], grad_skip


def solution(mesh):
    in_specs = (
        P("seq", "tp"),
        P("seq", "tp"),
        P(None, "seq", None),
        P("seq", "tp"),
        P("seq"),
        P("seq", "tp"),
        P("tp"),
        P("seq", "tp"),
    )
    out_specs = (P("seq", "tp"), P("seq", "tp"), P("seq", "tp"), P("seq"), P("tp"), P("seq", "tp"))
    return jax.shard_map(shards, mesh=mesh, in_specs=in_specs, out_specs=out_specs, check_vma=False)
```

time: 1200 us -> 217 us (0.18)
  local copies, waits for them, and re-layouts: 434 us -> 6.95 us
  other arithmetic: 359 us -> 4.56 us
  waiting for transfers between devices: 249 us -> 0 us
  Pallas kernels: 0 us -> 204 us
  matrix products: 128 us -> 0 us
  between operations: 14.4 us -> 0.7 us
    gather x14 -> x0, local copies, waits for them, and re-layouts: 333 us -> none  [the longest x2 91.1 us: shards(): preact = summed_pre + b_enc[index_table]]
    while x20 -> x0, other arithmetic: 253 us -> none
    pallas_call x0 -> x9, Pallas kernels: none -> 204 us  [the longest x2 49.6 us: pick(): pl.pallas_call(functools.partial(pick_kernel, bias is not None), grid=(TO...]
    dot_general x22 -> x0, matrix products: 128 us -> none  [the longest x4 39.9 us: grad_block(): lax.dot_general(slope_table, tok_rows, contract_rows, preferred_element_t...]
    all_gather x4 -> x0, waiting for transfers between devices: 99.1 us -> none  [the longest x1 52.1 us: shards(): all_tokens = lax.all_gather(inputs, 'seq', axis=0, tiled=True)]
    scatter-add x1 -> x0, other arithmetic: 89.5 us -> none  [shards(): jnp.zeros(b_enc.shape, jnp.float32).at[index_table.reshape(-1)]]
    reduce_scatter x2 -> x0, waiting for transfers between devices: 79.1 us -> none  [the longest x1 79.1 us: shards(): lax.psum_scatter(lax.map(decode_block, jnp.arange(row_count // sub_rows))...]
    psum x2 -> x0, waiting for transfers between devices: 68.6 us -> none  [the longest x1 68.6 us: shards(): summed_back = lax.psum(partial_back, 'tp')]
  transfers between devices with their start and end apart: 8 -> 0, of which waited for: 4 -> 0; matrix products, arithmetic and copies ran while one was open for 59% -> 0% of each run, Pallas kernels for 0% -> 0%
where the time goes in v1:
time: 217 us; the launch traced here: 216 us
  Pallas kernels  204 us (94%)
  local copies, waits for them, and re-layouts  6.95 us (3%)
  other arithmetic  4.56 us (2%)
    pallas_call x2, Pallas kernels, pick(): pl.pallas_call(functools.partial(pick_kernel, bias is not None), grid=(TO...  49.6 us
    pallas_call x1, Pallas kernels, residuals(): pl.pallas_call(residual_kernel, out_shape=[jax.ShapeDtypeStruct((ROWS, CO...  41.9 us
    pallas_call x1, Pallas kernels, grads(): pl.pallas_call(grad_kernel, grid=(FEATS // feats,), in_specs=[slots, slot...  31.3 us
    pallas_call x1, Pallas kernels, gather(): pl.pallas_call(gather_kernel, out_shape=[jax.ShapeDtypeStruct((TOKENS, CO...  29.4 us
    pallas_call x2, Pallas kernels, sum_tp(): pl.pallas_call(sum_kernel, out_shape=jax.ShapeDtypeStruct((SLOTS, TOKENS)...  24.1 us
    pallas_call x1, Pallas kernels, decode(): pl.pallas_call(decode_kernel, grid=(TOKENS // rows,), in_specs=[pl.BlockS...  20.4 us
    pallas_call x1, Pallas kernels, small_grads(): pl.pallas_call(small_kernel, in_specs=[pl.BlockSpec(memory_space=pltpu.VM...  7.21 us

profile of v1, /device:TPU:0, one launch (start us, length us, event | category | flops | bytes accessed | tf_op | source)
XLA Modules:
  0.0 216.1 jit_solution(17941732652745393543)
XLA Ops:
  0.7 1.3 broadcast_select_fusion
  2.0 1.5 multiply_select_fusion.key_ref
  3.5 0.8 bitcast_maximum_fusion
  4.3 0.9 multiply_select_fusion.1
  5.2 0.7 broadcast_in_dim.33.base_ref
  5.9 1.3 copy.17.key_ref
  7.2 0.1 broadcast_bitcast_fusion
  7.3 1.3 copy.16.id_ref
  8.6 1.6 broadcast_in_dim.36.base_ref
  10.2 29.4 %gather_inputs.1 = (bf16[2048,512]{1,0:T(8,128)(2,1)}, bf16[2048,256]{1,0:T(8,128)(2,1)}) custom-call(bf16[128,512]{1,0:T(8,128)(2,1)} %x_ref.1), custom_call_target="tpu_custom_call" | custom-call | tf_op jit(solution)/shard_map/gather_inputs/pallas_call | solution.py:219
  39.6 24.8 %encode.1.x_ref = f32[8,2048]{1,0:T(8,128)} custom-call(bf16[2048,512]{1,0:T(8,128)(2,1)} %get-tuple-element.15.x_ref, s32[2048,128]{1,0:T(8,128)} %copy.16.id_ref, bf16[4096,512]{1,0:T(8,128)(2,1)} %w_ref.3, f32[1,4096]{1,0:T(1,128)} %bitcast.17), custom_call_target="tpu_custom_call" | custom-call | tf_op jit(solution)/shard_map/encode/pallas_call | solution.py:275
  64.4 12.7 %sum_pre.1.pre_ref = f32[8,2048]{1,0:T(8,128)} custom-call(f32[8,2048]{1,0:T(8,128)} %encode.1.x_ref), custom_call_target="tpu_custom_call" | custom-call | tf_op jit(solution)/shard_map/sum_pre/pallas_call | solution.py:314
  77.1 20.4 %decode.1.part = f32[2048,512]{1,0:T(8,128)} custom-call(f32[2048,8]{1,0:T(8,128)} %copy.17.key_ref, f32[8,2048]{1,0:T(8,128)} %sum_pre.1.pre_ref, bf16[16,4096]{1,0:T(8,128)(2,1)} %broadcast_in_dim.33.base_ref, bf16[4096,512]{1,0:T(8,128)(2,1)} %w_ref.5, bf16[2048,256]{1,0:T(8,128)(2,1)} %get-tuple-element.16.xs_ref, bf16[256,512]{1,0:T(8,128)(2,1)} %ws_ref.1), custom_call_target="tpu_custom_call" | custom-call | tf_op jit(solution)/shard_map/decode/pallas_call | solution.py:354
  97.5 41.9 %residuals.1 = (bf16[128,512]{1,0:T(8,128)(2,1)}, bf16[2048,512]{1,0:T(8,128)(2,1)}) custom-call(f32[2048,512]{1,0:T(8,128)} %decode.1.part, bf16[128,512]{1,0:T(8,128)(2,1)} %target.1, f32[1,512]{1,0:T(1,128)} %bitcast.18), custom_call_target="tpu_custom_call" | custom-call | tf_op jit(solution)/shard_map/residuals/pallas_call | solution.py:440
  139.4 24.8 %backward.1.x_ref = f32[8,2048]{1,0:T(8,128)} custom-call(bf16[2048,512]{1,0:T(8,128)(2,1)} %get-tuple-element.18.x_ref.r_ref, s32[2048,128]{1,0:T(8,128)} %copy.16.id_ref, bf16[4096,512]{1,0:T(8,128)(2,1)} %w_ref.5), custom_call_target="tpu_custom_call" | custom-call | tf_op jit(solution)/shard_map/backward/pallas_call | solution.py:275
  164.2 11.4 %sum_back.1.back_ref = f32[8,2048]{1,0:T(8,128)} custom-call(f32[8,2048]{1,0:T(8,128)} %backward.1.x_ref), custom_call_target="tpu_custom_call" | custom-call | tf_op jit(solution)/shard_map/sum_back/pallas_call | solution.py:314
  175.6 0.0 copy-start
  175.6 7.2 %small_grads.1 = (f32[32,128]{1,0:T(8,128)}, bf16[256,512]{1,0:T(8,128)(2,1)}, f32[8,512]{1,0:T(8,128)}) custom-call(s32[8,2048]{1,0:T(8,128)} %bitcast.16, f32[8,2048]{1,0:T(8,128)} %sum_pre.1.pre_ref, f32[8,2048]{1,0:T(8,128)} %sum_back.1.back_ref, bf16[2048,256]{1,0:T(8,128)(2,1)} %get-tuple-element.16.xs_ref, bf16[2048,512]{1,0:T(8,128)(2,1)} %get-tuple-element.18.x_ref.r_ref), custom_call_target="tpu_custom_call" | custom-call | tf_op jit(solution)/shard_map/small_grads/pallas_call | solution.py:543
  182.8 1.3 slice.3
  184.1 31.3 %grads.1 = (bf16[4096,512]{1,0:T(8,128)(2,1)}, bf16[4096,512]{1,0:T(8,128)(2,1)}) custom-call(f32[8,2048]{1,0:T(8,128)} %multiply_select_fusion.key_ref, f32[8,2048]{1,0:T(8,128)} %sum_pre.1.pre_ref, f32[8,2048]{1,0:T(8,128)} %sum_back.1.back_ref, bf16[4096,128]{1,0:T(8,128)(2,1)} %broadcast_in_dim.36.base_ref, bf16[2048,512]{1,0:T(8,128)(2,1)} %get-tuple-element.15.x_ref, ...), custom_call_target="tpu_custom_call" | custom-call | tf_op jit(solution)/shard_map/grads/pallas_call | solution.py:501
  215.5 0.0 copy-done
  215.5 0.7 copy.20
  (1 shorter events, 0.0 us)
Async XLA Ops:
  175.6 39.9 %copy-start = (bf16[128,512]{1,0:T(8,128)(2,1)S(1)}, bf16[128,512]{1,0:T(8,128)(2,1)}, u32[]{:S(2)}) copy-start(bf16[128,512]{1,0:T(8,128)(2,1)} %get-tuple-element.30) | copy-start | bytes 393220

commit v2 on v1

v2 whole, which is shorter than its diff:
```python
import functools

import jax
import jax.numpy as jnp
from jax import lax
from jax.experimental import pallas as pl
from jax.experimental.pallas import tpu as pltpu
from jax.sharding import PartitionSpec as P

MESH = pl.DeviceIdType.MESH
BF16 = jnp.bfloat16
F32 = jnp.float32
VMEM_LIMIT = 56 << 20

N_SEQ = 16
N_TP = 8
ROWS = 128
TOKENS = 2048
COLS = 512
FEATS = 4096
SKIP = 256
SLOTS = 8


class Place:
    def __init__(self):
        self.s = lax.axis_index("seq")
        self.p = lax.axis_index("tp")
        s, p = self.s, self.p
        self.c = lax.rem(s, 2)
        self.y = lax.rem(lax.div(s, 2), 4)
        self.zh = lax.div(s, 8)
        self.x = lax.rem(p, 4)
        self.zl = lax.div(p, 4)
        self.mate = (s + 1 - 2 * self.c, p)
        self.up = (self.seq(0, 1), p)
        self.down = (self.seq(0, 3), p)
        self.far = (self.seq(1, 0), p)
        self.right = (s, self.tp(0, 1))
        self.left = (s, self.tp(0, 3))
        self.side = (s, self.tp(1, 0))

    def seq(self, b, dy, other_core=False):
        zh = 1 - self.zh if b else self.zh
        c = 1 - self.c if other_core else self.c
        return (zh * 4 + lax.rem(self.y + dy, 4)) * 2 + c

    def tp(self, b, dx):
        zl = 1 - self.zl if b else self.zl
        return zl * 4 + lax.rem(self.x + dx, 4)


def greet(devices):
    barrier = pltpu.get_barrier_semaphore()
    for dev in devices:
        pl.semaphore_signal(barrier, inc=1, device_id=dev, device_id_type=MESH)
    pl.semaphore_wait(barrier, len(devices))


class Sender:
    def __init__(self, send, recv, here):
        self.send, self.recv, self.here = send, recv, here

    def copy(self, i, src, dst, dev):
        return pltpu.make_async_remote_copy(
            src_ref=src, dst_ref=dst, send_sem=self.send.at[i], recv_sem=self.recv.at[i],
            device_id=dev, device_id_type=MESH,
        )

    def start(self, i, src, dst, dev):
        self.copy(i, src, dst, dev).start()

    def wait(self, i, dst):
        self.copy(i, dst, dst, self.here).wait_recv()

    def sent(self, i, like):
        self.copy(i, like, like, self.here).wait_send()


def choose(k, values):
    out = values[0]
    for i, v in enumerate(values[1:], 1):
        out = jnp.where(k == i, v, out)
    return out


def seq_rows(q, half=None):
    if half is None:
        return pl.ds(pl.multiple_of(q * ROWS, ROWS), ROWS)
    return pl.ds(pl.multiple_of(q * ROWS + half * (ROWS // 2), ROWS // 2), ROWS // 2)


def key_of(number):
    value = (128 + (number & 127)).astype(F32)
    for bit in range(5):
        value = value * jnp.where((number & (128 << bit)) != 0, float(2 ** (2**bit)), 1.0)
    return value


PAIR = 2 * ROWS
PICK_ORDER = ((0, 0), (0, 3), (0, 1), (1, 0), (0, 2), (1, 3), (1, 1), (1, 2))
SEQ_KINDS = 19
HALVES = (2, 3, 6, 7, 12, 13, 17, 18)


def pick_slots(rows, w_ref, ids, bias):
    width = 256
    accs = [jnp.zeros((8, PAIR), F32) for _ in range(SLOTS)]
    for c in range(FEATS // width):
        lines = slice(c * width, (c + 1) * width)
        dots = lax.dot_general(
            w_ref[lines, :], rows, (((1,), (1,)), ((), ())), preferred_element_type=F32
        )
        if bias is not None:
            dots = dots + jnp.concatenate([bias[lines, :]] * 2, axis=1)
        for j in range(SLOTS):
            row = ids[j : j + 1, :]
            tree = dots
            for bit in range(4, -1, -1):
                half = tree.shape[0] // 2
                upper = jnp.broadcast_to((row & (8 << bit)) != 0, (half, PAIR))
                tree = jnp.where(upper, tree[half:], tree[:half])
            here = jnp.broadcast_to((row >> 8) == c, (8, PAIR))
            accs[j] = jnp.where(here, tree, accs[j])
    line = lax.broadcasted_iota(jnp.int32, (8, PAIR), 0)
    out = []
    for j in range(SLOTS):
        hit = line == (ids[j : j + 1, :] & 7)
        out.append(jnp.sum(jnp.where(hit, accs[j], 0.0), axis=0, keepdims=True))
    return jnp.concatenate(out, axis=0)


def gather_and_pick(at, net, pnet, own, rows_ref, w_ref, id_ref, bias, parts, out_ref, keep, extra):
    def blk(b, dy, half=None, other=False):
        return rows_ref.at[seq_rows(at.seq(b, dy, other), half)]

    mine = rows_ref.at[seq_rows(at.s)]
    net.start(9, own, mine, at.mate)
    net.start(8, own, mine, at.far)
    net.start(0, own, mine, at.up)
    net.start(1, own, mine, at.down)
    extra(0)
    keep()
    net.wait(9, blk(0, 0, None, True))

    def ring(b):
        k, m = 4 * b, 9 + 5 * b
        net.wait(k, blk(b, 3))
        net.start(k + 2, blk(b, 3, 0), blk(b, 3, 0), at.up)
        net.start(m + 1, blk(b, 3), blk(b, 3), at.mate)
        net.wait(k + 1, blk(b, 1))
        net.start(k + 3, blk(b, 1, 1), blk(b, 1, 1), at.down)
        net.start(m + 2, blk(b, 1), blk(b, 1), at.mate)

    def last(b):
        k, m = 4 * b, 9 + 5 * b
        net.wait(k + 2, blk(b, 2, 0))
        net.start(m + 3, blk(b, 2, 0), blk(b, 2, 0), at.mate)
        net.wait(k + 3, blk(b, 2, 1))
        net.start(m + 4, blk(b, 2, 1), blk(b, 2, 1), at.mate)

    def step(i):
        if i == 1:
            ring(0)
            net.wait(8, blk(1, 0))
            net.start(4, blk(1, 0), blk(1, 0), at.up)
            net.start(5, blk(1, 0), blk(1, 0), at.down)
            net.start(14, blk(1, 0), blk(1, 0), at.mate)
            net.wait(10, blk(0, 3, None, True))
        if i == 2:
            net.wait(11, blk(0, 1, None, True))
        if i == 3:
            ring(1)
            last(0)
            net.wait(14, blk(1, 0, None, True))
        if i == 4:
            net.wait(12, blk(0, 2, 0, True))
            net.wait(13, blk(0, 2, 1, True))
        if i == 5:
            last(1)
            net.wait(15, blk(1, 3, None, True))
        if i == 6:
            net.wait(16, blk(1, 1, None, True))
        if i == 7:
            net.wait(17, blk(1, 2, 0, True))
            net.wait(18, blk(1, 2, 1, True))
        extra(i)

    def pair_of(k):
        return choose(k, [lax.div(at.seq(b, dy), 2) for b, dy in PICK_ORDER])

    def lanes(k):
        return pl.ds(pl.multiple_of(pair_of(k) * PAIR, PAIR), PAIR)

    def body(k, carry):
        for i in range(1, 8):
            pl.when(k == i)(functools.partial(step, i))
        q = pair_of(k)
        rows = rows_ref[pl.ds(pl.multiple_of(q * PAIR, PAIR), PAIR), :]
        parts[k, at.p] = pick_slots(rows, w_ref, id_ref[:, lanes(k)], bias)
        for d in range(1, N_TP):
            here = parts.at[k, at.p]
            pnet.start((k, d), here, here, (at.s, lax.rem(at.p + d, N_TP)))
        return carry

    lax.fori_loop(0, 8, body, 0)
    extra(8)

    def add_up(k, carry):
        for d in range(1, N_TP):
            pnet.wait((k, d), parts.at[k, lax.rem(at.p + N_TP - d, N_TP)])
        total = parts[k, 0]
        for q in range(1, N_TP):
            total = total + parts[k, q]
        out_ref[:, lanes(k)] = total
        return carry

    lax.fori_loop(0, 8, add_up, 0)
    for i in range(SEQ_KINDS):
        net.sent(i, rows_ref.at[pl.ds(0, ROWS // 2 if i in HALVES else ROWS)])

    def done(k, carry):
        for d in range(1, N_TP):
            pnet.sent((k, d), parts.at[k, at.p])
        return carry

    lax.fori_loop(0, 8, done, 0)


def encode_kernel(
    x_ref, id_ref, w_hbm, b_ref, all_ref, skip_ref, pre_ref, w_ref, bias, parts,
    send, recv, psend, precv, send2, recv2, local,
):
    at = Place()
    here = (at.s, at.p)
    load = pltpu.make_async_copy(w_hbm, w_ref, local.at[0])
    load.start()
    own = pltpu.make_async_copy(x_ref, all_ref.at[seq_rows(at.s)], local.at[1])
    own.start()

    half_p = lax.div(at.s, 2)
    stay = half_p == at.p
    peers = [(at.s, lax.rem(at.p + d, N_TP)) for d in range(1, N_TP)]
    same, cross = (2 * at.p + at.c, half_p), (2 * at.p + 1 - at.c, half_p)
    around = [at.mate, at.up, at.down, at.far, cross] + peers
    barrier = pltpu.get_barrier_semaphore()
    for dev in around:
        pl.semaphore_signal(barrier, inc=1, device_id=dev, device_id_type=MESH)

    @pl.when(jnp.logical_not(stay))
    def _():
        pl.semaphore_signal(barrier, inc=1, device_id=same, device_id_type=MESH)

    first = lax.axis_index("tp") == 0
    for g in range(FEATS // 128):
        row = jnp.where(first, b_ref[g : g + 1, :], 0.0)
        bias[g * 128 : (g + 1) * 128, :] = jnp.broadcast_to(row, (128, 128)).T
    pl.semaphore_wait(barrier, len(around) + 1 - stay.astype(jnp.int32))

    net, pnet, net2 = Sender(send, recv, here), Sender2(psend, precv, here), Sender(send2, recv2, here)

    def part(h):
        return x_ref.at[:, pl.ds(pl.multiple_of(h * SKIP, SKIP), SKIP)]

    land = skip_ref.at[seq_rows(at.s)]
    inside = pltpu.make_async_copy(part(at.c), land, local.at[2])

    def piece(b, dx, half=None):
        q = at.tp(b, dx)
        if half is None:
            return skip_ref.at[pl.ds(pl.multiple_of(q * 256, 256), 256)]
        return skip_ref.at[pl.ds(pl.multiple_of(q * 256 + half * 128, 128), 128)]

    def ring(b):
        k = 2 + 4 * b
        net2.wait(k, piece(b, 3))
        net2.start(k + 2, piece(b, 3, 0), piece(b, 3, 0), at.right)
        net2.wait(k + 1, piece(b, 1))
        net2.start(k + 3, piece(b, 1, 1), piece(b, 1, 1), at.left)

    def extra(i):
        if i == 0:
            net2.start(1, part(1 - at.c), land, cross)

            @pl.when(jnp.logical_not(stay))
            def _():
                net2.start(0, part(at.c), land, same)

            @pl.when(stay)
            def _():
                inside.start()

        if i == 1:
            net2.wait(1, skip_ref.at[seq_rows(2 * at.p + 1 - at.c)])

            @pl.when(jnp.logical_not(stay))
            def _():
                net2.wait(0, skip_ref.at[seq_rows(2 * at.p + at.c)])

            @pl.when(stay)
            def _():
                pltpu.make_async_copy(part(at.c), land, local.at[2]).wait()

            net2.start(10, piece(0, 0), piece(0, 0), at.side)
            net2.start(2, piece(0, 0), piece(0, 0), at.right)
            net2.start(3, piece(0, 0), piece(0, 0), at.left)
        if i == 3:
            net2.wait(10, piece(1, 0))
            net2.start(6, piece(1, 0), piece(1, 0), at.right)
            net2.start(7, piece(1, 0), piece(1, 0), at.left)
            ring(0)
        if i == 5:
            ring(1)
        if i == 8:
            for b in (0, 1):
                net2.wait(4 + 4 * b, piece(b, 2, 0))
                net2.wait(5 + 4 * b, piece(b, 2, 1))

    def keep():
        load.wait()
        own.wait()

    gather_and_pick(at, net, pnet, x_ref, all_ref, w_ref, id_ref, bias, parts, pre_ref, keep, extra)

    @pl.when(jnp.logical_not(stay))
    def _():
        net2.sent(0, land)

    net2.sent(1, land)
    for i in range(2, 11):
        net2.sent(i, skip_ref.at[pl.ds(0, 128 if i in (4, 5, 8, 9) else 256)])


class Sender2(Sender):
    def copy(self, i, src, dst, dev):
        return pltpu.make_async_remote_copy(
            src_ref=src, dst_ref=dst, send_sem=self.send.at[i[0], i[1]],
            recv_sem=self.recv.at[i[0], i[1]], device_id=dev, device_id_type=MESH,
        )


def encode(x, ids, w, bias):
    vm = pl.BlockSpec(memory_space=pltpu.VMEM)
    hbm = pl.BlockSpec(memory_space=pl.ANY)
    dma = pltpu.SemaphoreType.DMA
    return pl.pallas_call(
        encode_kernel,
        out_shape=[
            jax.ShapeDtypeStruct((TOKENS, COLS), BF16),
            jax.ShapeDtypeStruct((TOKENS, SKIP), BF16),
            jax.ShapeDtypeStruct((SLOTS, TOKENS), F32),
        ],
        in_specs=[hbm, vm, hbm, vm],
        out_specs=[vm, vm, vm],
        scratch_shapes=[
            pltpu.VMEM((FEATS, COLS), BF16),
            pltpu.VMEM((FEATS, 128), F32),
            pltpu.VMEM((8, N_TP, SLOTS, PAIR), F32),
            dma((SEQ_KINDS,)), dma((SEQ_KINDS,)), dma((8, N_TP)), dma((8, N_TP)),
            dma((11,)), dma((11,)), dma((3,)),
        ],
        compiler_params=pltpu.CompilerParams(
            collective_id=0, has_side_effects=True, vmem_limit_bytes=VMEM_LIMIT
        ),
        name="encode",
    )(x, ids, w, bias)


SUM_ORDER = tuple((b, dy) for b in (1, 0) for dy in (2, 1, 3, 0))
SLAB = 32


def residual_kernel(
    pre_ref, id_ref, w_hbm, xs_ref, ws_ref, target, bias, recon, all_ref, back_ref,
    w_ref, base, table, turned, part, mrecv, out_buf, half_in, full_in, far_out, far_in, res, parts,
    msend, mrcv, ysend, yrcv, send, recv, psend, precv, local,
):
    at = Place()
    here = (at.s, at.p)
    load = pltpu.make_async_copy(w_hbm, w_ref, local.at[0])
    load.start()
    peers = [(at.s, lax.rem(at.p + d, N_TP)) for d in range(1, N_TP)]
    around = [at.mate, at.up, at.down, at.far] + peers
    barrier = pltpu.get_barrier_semaphore()
    for dev in around:
        pl.semaphore_signal(barrier, inc=1, device_id=dev, device_id_type=MESH)
    base[...] = key_of(lax.broadcasted_iota(jnp.int32, (SLAB, FEATS), 1)).astype(BF16)
    pl.semaphore_wait(barrier, len(around))
    load.wait()

    mnet, ynet = Sender(msend, mrcv, here), Sender(ysend, yrcv, here)
    H = ROWS // 2

    def pair(k, half=None):
        b, dy = SUM_ORDER[k]
        rows = seq_rows(at.seq(b, dy), half)
        mine = slice(0, ROWS) if half is None else slice(half * H, (half + 1) * H)
        return part[rows, :] + mrecv[k, mine, :]

    def opposite(i):
        mnet.wait(4 * i, mrecv.at[4 * i])
        out_buf[3 * i] = pair(4 * i).astype(BF16)
        ynet.start(4 * i, out_buf.at[3 * i, pl.ds(0, H)], half_in.at[2 * i], at.up)
        ynet.start(4 * i + 1, out_buf.at[3 * i, pl.ds(H, H)], half_in.at[2 * i + 1], at.down)

    def upward(i):
        k = 4 * i + 1
        mnet.wait(k, mrecv.at[k])
        out_buf[3 * i + 1, H:, :] = pair(k, 1).astype(BF16)
        ynet.wait(4 * i, half_in.at[2 * i])
        out_buf[3 * i + 1, :H, :] = (pair(k, 0) + half_in[2 * i].astype(F32)).astype(BF16)
        ynet.start(4 * i + 2, out_buf.at[3 * i + 1], full_in.at[2 * i], at.up)

    def downward(i):
        k = 4 * i + 2
        mnet.wait(k, mrecv.at[k])
        out_buf[3 * i + 2, :H, :] = pair(k, 0).astype(BF16)
        ynet.wait(4 * i + 1, half_in.at[2 * i + 1])
        out_buf[3 * i + 2, H:, :] = (pair(k, 1) + half_in[2 * i + 1].astype(F32)).astype(BF16)
        ynet.start(4 * i + 3, out_buf.at[3 * i + 2], full_in.at[2 * i + 1], at.down)

    def here_sum(i):
        k = 4 * i + 3
        mnet.wait(k, mrecv.at[k])
        ynet.wait(4 * i + 2, full_in.at[2 * i])
        ynet.wait(4 * i + 3, full_in.at[2 * i + 1])
        return pair(k) + full_in[2 * i].astype(F32) + full_in[2 * i + 1].astype(F32)

    def step(i):
        if i == 1:
            opposite(0)
        if i == 2:
            upward(0)
        if i == 3:
            downward(0)
        if i == 5:
            opposite(1)
            far_out[...] = here_sum(0)
            ynet.start(8, far_out, far_in, at.far)
        if i == 6:
            upward(1)
        if i == 7:
            downward(1)

    filler = jnp.zeros((128 - 2 * SLOTS, 128), F32)

    def body(k, carry):
        q = choose(k, [lax.div(at.seq(b, dy), 2) for b, dy in SUM_ORDER])
        first = pl.multiple_of(q * PAIR, PAIR)
        for t in range(2):
            lanes = pl.ds(pl.multiple_of(first + t * 128, 128), 128)
            ids = id_ref[:, lanes]
            act = jnp.maximum(pre_ref[:, lanes], 0.0)
            key = jnp.where(ids >= 0, key_of(ids), -1.0)
            turned[t * 128 : (t + 1) * 128, :] = jnp.concatenate([act, key, filler], axis=0).T

        def slab(r, carry2):
            line = pl.ds(pl.multiple_of(r * SLAB, SLAB), SLAB)
            both = turned[line, :]
            keys, vals = [], []
            for j in range(SLOTS):
                keys.append(jnp.broadcast_to(both[:, SLOTS + j : SLOTS + j + 1], (SLAB, 128)).astype(BF16))
                vals.append(jnp.broadcast_to(both[:, j : j + 1], (SLAB, 128)).astype(BF16))
            for g in range(FEATS // 128):
                spot = base[:, g * 128 : (g + 1) * 128]
                acc = jnp.zeros((SLAB, 128), BF16)
                for j in range(SLOTS):
                    acc = jnp.where(keys[j] == spot, vals[j], acc)
                table[line, g * 128 : (g + 1) * 128] = acc
            return carry2

        lax.fori_loop(0, PAIR // SLAB, slab, 0)
        rows = pl.ds(first, PAIR)
        part[rows, :] = jnp.dot(table[...], w_ref[...], preferred_element_type=F32) + jnp.dot(
            xs_ref[rows, :], ws_ref[...], preferred_element_type=F32
        )
        mnet.start(k, part.at[seq_rows(2 * q + 1 - at.c)], mrecv.at[k], at.mate)
        for i in range(1, 8):
            pl.when(k == i)(functools.partial(step, i))
        return carry

    lax.fori_loop(0, 8, body, 0)
    total = here_sum(1) + bias[...]
    ynet.wait(8, far_in)
    total = total + far_in[...]
    recon[...] = total.astype(BF16)
    res[...] = (total - target[...].astype(F32)).astype(BF16)
    own = pltpu.make_async_copy(res, all_ref.at[seq_rows(at.s)], local.at[1])
    own.start()
    net, pnet = Sender(send, recv, here), Sender2(psend, precv, here)
    gather_and_pick(
        at, net, pnet, res, all_ref, w_ref, id_ref, None, parts, back_ref, own.wait, lambda i: None
    )
    for k in range(8):
        mnet.sent(k, mrecv.at[k])
    for i in (0, 1):
        ynet.sent(4 * i, half_in.at[0])
        ynet.sent(4 * i + 1, half_in.at[0])
        ynet.sent(4 * i + 2, full_in.at[0])
        ynet.sent(4 * i + 3, full_in.at[0])
    ynet.sent(8, far_out)


def residuals(pre, ids, w, xs, ws, target, bias):
    vm = pl.BlockSpec(memory_space=pltpu.VMEM)
    hbm = pl.BlockSpec(memory_space=pl.ANY)
    dma = pltpu.SemaphoreType.DMA
    return pl.pallas_call(
        residual_kernel,
        out_shape=[
            jax.ShapeDtypeStruct((ROWS, COLS), BF16),
            jax.ShapeDtypeStruct((TOKENS, COLS), BF16),
            jax.ShapeDtypeStruct((SLOTS, TOKENS), F32),
        ],
        in_specs=[vm, vm, hbm, vm, vm, vm, vm],
        out_specs=[vm, vm, vm],
        scratch_shapes=[
            pltpu.VMEM((FEATS, COLS), BF16),
            pltpu.VMEM((SLAB, FEATS), BF16),
            pltpu.VMEM((PAIR, FEATS), BF16),
            pltpu.VMEM((PAIR, 128), F32),
            pltpu.VMEM((TOKENS, COLS), F32),
            pltpu.VMEM((8, ROWS, COLS), F32),
            pltpu.VMEM((6, ROWS, COLS), BF16),
            pltpu.VMEM((4, ROWS // 2, COLS), BF16),
            pltpu.VMEM((4, ROWS, COLS), BF16),
            pltpu.VMEM((ROWS, COLS), F32),
            pltpu.VMEM((ROWS, COLS), F32),
            pltpu.VMEM((ROWS, COLS), BF16),
            pltpu.VMEM((8, N_TP, SLOTS, PAIR), F32),
            dma((8,)), dma((8,)), dma((9,)), dma((9,)),
            dma((SEQ_KINDS,)), dma((SEQ_KINDS,)), dma((8, N_TP)), dma((8, N_TP)), dma((2,)),
        ],
        compiler_params=pltpu.CompilerParams(
            collective_id=1, has_side_effects=True, vmem_limit_bytes=VMEM_LIMIT
        ),
        name="residuals",
    )(pre, ids, w, xs, ws, target, bias)


def grad_kernel(
    id_ref, pre_ref, back_ref, x_ref, r_ref, ge_ref, gd_ref, st_ref, at_ref, base_ref
):
    feats = base_ref.shape[0]
    number = pl.program_id(0) * feats + lax.broadcasted_iota(jnp.int32, (feats, 128), 0)
    base_ref[...] = key_of(number).astype(BF16)
    for t in range(TOKENS // 128):
        lanes = slice(t * 128, (t + 1) * 128)
        pre = pre_ref[:, lanes]
        slope = jnp.where(pre > 0.0, back_ref[:, lanes], 0.0)
        act = jnp.maximum(pre, 0.0)
        ids = id_ref[:, lanes]
        key = jnp.where(ids >= 0, key_of(ids), -1.0)
        keys, slopes, acts = [], [], []
        for j in range(SLOTS):
            row = slice(j, j + 1)
            keys.append(jnp.broadcast_to(key[row, :], (16, 128)).astype(BF16))
            slopes.append(jnp.broadcast_to(slope[row, :], (16, 128)).astype(BF16))
            acts.append(jnp.broadcast_to(act[row, :], (16, 128)).astype(BF16))
        for r in range(feats // 16):
            lines = slice(r * 16, (r + 1) * 16)
            base = base_ref[lines, :]
            s_acc = jnp.zeros((16, 128), BF16)
            a_acc = jnp.zeros((16, 128), BF16)
            for j in range(SLOTS):
                hit = keys[j] == base
                s_acc = jnp.where(hit, slopes[j], s_acc)
                a_acc = jnp.where(hit, acts[j], a_acc)
            st_ref[lines, lanes] = s_acc
            at_ref[lines, lanes] = a_acc
    ge_ref[...] = jnp.dot(st_ref[...], x_ref[...], preferred_element_type=F32).astype(BF16)
    gd_ref[...] = jnp.dot(at_ref[...], r_ref[...], preferred_element_type=F32).astype(BF16)


def grads(ids, pre, back, x, r, feats=512):
    slots = pl.BlockSpec((SLOTS, TOKENS), lambda i: (0, 0))
    whole = pl.BlockSpec((TOKENS, COLS), lambda i: (0, 0))
    out = pl.BlockSpec((feats, COLS), lambda i: (i, 0))
    return pl.pallas_call(
        grad_kernel,
        grid=(FEATS // feats,),
        in_specs=[slots, slots, slots, whole, whole],
        out_specs=[out, out],
        out_shape=[jax.ShapeDtypeStruct((FEATS, COLS), BF16)] * 2,
        scratch_shapes=[pltpu.VMEM((feats, TOKENS), BF16)] * 2 + [pltpu.VMEM((feats, 128), BF16)],
        compiler_params=pltpu.CompilerParams(vmem_limit_bytes=VMEM_LIMIT),
        name="grads",
    )(ids, pre, back, x, r)


def small_kernel(id_ref, pre_ref, back_ref, xs_ref, r_ref, gb_ref, gs_ref, bd_ref):
    total = jnp.zeros((FEATS // 128, 128), F32)
    contract = (((0,), (0,)), ((), ()))
    pairs = (((1,), (1,)), ((), ()))
    for t in range(TOKENS // 512):
        lanes = slice(t * 512, (t + 1) * 512)
        ids = id_ref[:, lanes]
        high, low = ids >> 7, ids & 127
        slope = jnp.where(pre_ref[:, lanes] > 0.0, back_ref[:, lanes], 0.0)
        top = slope.astype(BF16).astype(F32)
        rest = slope - top
        rest_top = rest.astype(BF16).astype(F32)
        last = rest - rest_top
        lines = lax.broadcasted_iota(jnp.int32, (FEATS // 128, 512), 0)
        lanes128 = lax.broadcasted_iota(jnp.int32, (128, 512), 0)
        for j in range(SLOTS):
            row = slice(j, j + 1)
            one = jnp.where(high[row, :] == lines, 1.0, 0.0).astype(BF16)
            hit = low[row, :] == lanes128
            for value in (top, rest_top, last):
                table = jnp.where(hit, value[row, :], 0.0).astype(BF16)
                total += lax.dot_general(one, table, pairs, preferred_element_type=F32)
    gb_ref[...] = total
    gs_ref[...] = lax.dot_general(
        xs_ref[...], r_ref[...], contract, preferred_element_type=F32
    ).astype(BF16)
    bd_ref[...] = jnp.dot(jnp.ones((8, TOKENS), BF16), r_ref[...], preferred_element_type=F32)


def small_grads(ids, pre, back, xs, r):
    return pl.pallas_call(
        small_kernel,
        in_specs=[pl.BlockSpec(memory_space=pltpu.VMEM)] * 5,
        out_specs=[pl.BlockSpec(memory_space=pltpu.VMEM)] * 3,
        out_shape=[
            jax.ShapeDtypeStruct((FEATS // 128, 128), F32),
            jax.ShapeDtypeStruct((SKIP, COLS), BF16),
            jax.ShapeDtypeStruct((8, COLS), F32),
        ],
        compiler_params=pltpu.CompilerParams(vmem_limit_bytes=VMEM_LIMIT),
        name="small_grads",
    )(ids, pre, back, xs, r)


def shards(inputs, target, feature_slots, w_enc, b_enc, w_dec, b_dec, w_skip):
    ids = feature_slots[:, 0, :].T
    all_x, x_skip, pre = encode(inputs, ids, w_enc, b_enc.reshape(FEATS // 128, 128))
    recon, all_r, back = residuals(pre, ids, w_dec, x_skip, w_skip, target, b_dec[None, :])
    grad_enc, grad_dec = grads(ids, pre, back, all_x, all_r)
    grad_benc, grad_skip, grad_bdec = small_grads(ids, pre, back, x_skip, all_r)
    return recon, grad_enc, grad_dec, grad_benc.reshape(-1), grad_bdec[0], grad_skip


def solution(mesh):
    in_specs = (
        P("seq", "tp"),
        P("seq", "tp"),
        P(None, "seq", None),
        P("seq", "tp"),
        P("seq"),
        P("seq", "tp"),
        P("tp"),
        P("seq", "tp"),
    )
    out_specs = (P("seq", "tp"), P("seq", "tp"), P("seq", "tp"), P("seq"), P("tp"), P("seq", "tp"))
    return jax.shard_map(shards, mesh=mesh, in_specs=in_specs, out_specs=out_specs, check_vma=False)
```

time: 217 us -> 169 us (0.78)
  Pallas kernels: 204 us -> 165 us
  local copies, waits for them, and re-layouts: 6.95 us -> 1.96 us
  other arithmetic: 4.56 us -> 0 us
    pallas_call x6 -> x1, Pallas kernels: 123 us -> 45.7 us  [encode(): pl.pallas_call(encode_kernel, out_shape=[jax.ShapeDtypeStruct((TOKENS, CO...]
    pallas_call x1, Pallas kernels: 41.9 us -> 69.8 us  [residuals(): pl.pallas_call(residual_kernel, out_shape=[jax.ShapeDtypeStruct((ROWS, CO...]
    pallas_call x1, Pallas kernels: 31.3 us -> 42.3 us  [grads(): pl.pallas_call(grad_kernel, grid=(FEATS // feats,), in_specs=[slots, slot...]
    select_n x3 -> x0, other arithmetic: 3.71 us -> none  [the longest x1 1.5 us: shards(): key_t = jnp.where(ids_t >= 0, key_of(jnp.maximum(ids_t, 0)), -1.0)]
    broadcast_in_dim x2 -> x0, local copies, waits for them, and re-layouts: 2.26 us -> none  [the longest x1 1.59 us: shards(): base_col = jnp.broadcast_to(base[:, None], (FEATS, 128))]
where the time goes in v2:
time: 169 us; the launch traced here: 168 us
  Pallas kernels  165 us (98%)
  local copies, waits for them, and re-layouts  1.96 us (1%)
    pallas_call x1, Pallas kernels, residuals(): pl.pallas_call(residual_kernel, out_shape=[jax.ShapeDtypeStruct((ROWS, CO...  69.8 us
    pallas_call x1, Pallas kernels, encode(): pl.pallas_call(encode_kernel, out_shape=[jax.ShapeDtypeStruct((TOKENS, CO...  45.7 us
    pallas_call x1, Pallas kernels, grads(): pl.pallas_call(grad_kernel, grid=(FEATS // feats,), in_specs=[slots, slot...  42.3 us
    pallas_call x1, Pallas kernels, small_grads(): pl.pallas_call(small_kernel, in_specs=[pl.BlockSpec(memory_space=pltpu.VM...  7.21 us

profile of v2, /device:TPU:0, one launch (start us, length us, event | category | flops | bytes accessed | tf_op | source)
XLA Modules:
  0.0 167.6 jit_solution(14496145797840801819)
XLA Ops:
  0.6 45.7 %encode.1 = (bf16[2048,512]{1,0:T(8,128)(2,1)}, bf16[2048,256]{1,0:T(8,128)(2,1)}, f32[8,2048]{1,0:T(8,128)}) custom-call(bf16[128,512]{1,0:T(8,128)(2,1)} %x_ref.1, s32[8,2048]{1,0:T(8,128)} %bitcast.7, bf16[4096,512]{1,0:T(8,128)(2,1)} %w_hbm.2, f32[32,128]{1,0:T(8,128)} %bitcast.11), custom_call_target="tpu_custom_call" | custom-call | tf_op jit(solution)/shard_map/encode/pallas_call | solution.py:346
  46.3 69.8 %residuals.1 = (bf16[128,512]{1,0:T(8,128)(2,1)}, bf16[2048,512]{1,0:T(8,128)(2,1)}, f32[8,2048]{1,0:T(8,128)}) custom-call(f32[8,2048]{1,0:T(8,128)} %get-tuple-element.17.pre_ref, s32[8,2048]{1,0:T(8,128)} %bitcast.8, bf16[4096,512]{1,0:T(8,128)(2,1)} %w_hbm.3, bf16[2048,256]{1,0:T(8,128)(2,1)} %get-tuple-element.18.xs_ref, bf16[256,512]{1,0:T(8,128)(2,1)} %ws_ref.1, ...), custom_call_target="tpu_custom_call" | custom-call | tf_op jit(solution)/shard_map/residuals/pallas_call | solution.py:508
  116.2 0.0 copy-start
  116.2 7.2 %small_grads.1 = (f32[32,128]{1,0:T(8,128)}, bf16[256,512]{1,0:T(8,128)(2,1)}, f32[8,512]{1,0:T(8,128)}) custom-call(s32[8,2048]{1,0:T(8,128)} %bitcast.9, f32[8,2048]{1,0:T(8,128)} %get-tuple-element.17.pre_ref, f32[8,2048]{1,0:T(8,128)} %get-tuple-element.20.back_ref, bf16[2048,256]{1,0:T(8,128)(2,1)} %get-tuple-element.18.xs_ref, ...), custom_call_target="tpu_custom_call" | custom-call | tf_op jit(solution)/shard_map/small_grads/pallas_call | solution.py:621
  123.4 1.3 slice.3
  124.7 42.3 %grads.1 = (bf16[4096,512]{1,0:T(8,128)(2,1)}, bf16[4096,512]{1,0:T(8,128)(2,1)}) custom-call(s32[8,2048]{1,0:T(8,128)} %bitcast.10, f32[8,2048]{1,0:T(8,128)} %get-tuple-element.17.pre_ref, f32[8,2048]{1,0:T(8,128)} %get-tuple-element.20.back_ref, bf16[2048,512]{1,0:T(8,128)(2,1)} %get-tuple-element.21.x_ref, bf16[2048,512]{1,0:T(8,128)(2,1)} %get-tuple-element.22.r_ref), custom_call_target="tpu_custom_call" | custom-call | tf_op jit(solution)/shard_map/grads/pallas_call | solution.py:579
  166.9 0.0 copy-done
  166.9 0.7 copy.15
Async XLA Ops:
  116.2 50.8 %copy-start = (bf16[128,512]{1,0:T(8,128)(2,1)S(1)}, bf16[128,512]{1,0:T(8,128)(2,1)}, u32[]{:S(2)}) copy-start(bf16[128,512]{1,0:T(8,128)(2,1)} %get-tuple-element.34) | copy-start | bytes 393220

commit v3 on v2

--- a/solution.py
+++ b/solution.py
@@ -228,7 +228,7 @@
 
 
 def encode_kernel(
-    x_ref, id_ref, w_hbm, b_ref, all_ref, skip_ref, pre_ref, w_ref, bias, parts,
+    x_ref, id_ref, w_hbm, b_ref, all_ref, skip_ref, pre_ref, base_row, base_col, w_ref, bias, parts,
     send, recv, psend, precv, send2, recv2, local,
 ):
     at = Place()
@@ -251,8 +251,12 @@
     def _():
         pl.semaphore_signal(barrier, inc=1, device_id=same, device_id_type=MESH)
 
+    across = (128 + lax.broadcasted_iota(jnp.int32, (SLAB, 128), 1)).astype(F32)
+    below = (128 + lax.broadcasted_iota(jnp.int32, (128, 128), 0)).astype(F32)
     first = lax.axis_index("tp") == 0
     for g in range(FEATS // 128):
+        base_row[:, g * 128 : (g + 1) * 128] = (across * float(2**g)).astype(BF16)
+        base_col[g * 128 : (g + 1) * 128, :] = (below * float(2**g)).astype(BF16)
         row = jnp.where(first, b_ref[g : g + 1, :], 0.0)
         bias[g * 128 : (g + 1) * 128, :] = jnp.broadcast_to(row, (128, 128)).T
     pl.semaphore_wait(barrier, len(around) + 1 - stay.astype(jnp.int32))
@@ -290,7 +294,7 @@
             def _():
                 inside.start()
 
-        if i == 1:
+        if i == 2:
             net2.wait(1, skip_ref.at[seq_rows(2 * at.p + 1 - at.c)])
 
             @pl.when(jnp.logical_not(stay))
@@ -304,12 +308,12 @@
             net2.start(10, piece(0, 0), piece(0, 0), at.side)
             net2.start(2, piece(0, 0), piece(0, 0), at.right)
             net2.start(3, piece(0, 0), piece(0, 0), at.left)
-        if i == 3:
+        if i == 4:
             net2.wait(10, piece(1, 0))
             net2.start(6, piece(1, 0), piece(1, 0), at.right)
             net2.start(7, piece(1, 0), piece(1, 0), at.left)
             ring(0)
-        if i == 5:
+        if i == 6:
             ring(1)
         if i == 8:
             for b in (0, 1):
@@ -349,9 +353,11 @@
             jax.ShapeDtypeStruct((TOKENS, COLS), BF16),
             jax.ShapeDtypeStruct((TOKENS, SKIP), BF16),
             jax.ShapeDtypeStruct((SLOTS, TOKENS), F32),
+            jax.ShapeDtypeStruct((SLAB, FEATS), BF16),
+            jax.ShapeDtypeStruct((FEATS, 128), BF16),
         ],
         in_specs=[hbm, vm, hbm, vm],
-        out_specs=[vm, vm, vm],
+        out_specs=[vm] * 5,
         scratch_shapes=[
             pltpu.VMEM((FEATS, COLS), BF16),
             pltpu.VMEM((FEATS, 128), F32),
@@ -371,8 +377,8 @@
 
 
 def residual_kernel(
-    pre_ref, id_ref, w_hbm, xs_ref, ws_ref, target, bias, recon, all_ref, back_ref,
-    w_ref, base, table, turned, part, mrecv, out_buf, half_in, full_in, far_out, far_in, res, parts,
+    pre_ref, id_ref, w_hbm, xs_ref, ws_ref, target, bias, base, recon, all_ref, back_ref, skip_grad,
+    bias_grad, w_ref, table, turned, part, mrecv, out_buf, half_in, full_in, far_out, far_in, res, parts,
     msend, mrcv, ysend, yrcv, send, recv, psend, precv, local,
 ):
     at = Place()
@@ -384,7 +390,6 @@
     barrier = pltpu.get_barrier_semaphore()
     for dev in around:
         pl.semaphore_signal(barrier, inc=1, device_id=dev, device_id_type=MESH)
-    base[...] = key_of(lax.broadcasted_iota(jnp.int32, (SLAB, FEATS), 1)).astype(BF16)
     pl.semaphore_wait(barrier, len(around))
     load.wait()
 
@@ -488,8 +493,17 @@
     own = pltpu.make_async_copy(res, all_ref.at[seq_rows(at.s)], local.at[1])
     own.start()
     net, pnet = Sender(send, recv, here), Sender2(psend, precv, here)
+
+    def extra(i):
+        if i == 8:
+            skip_grad[...] = lax.dot_general(
+                xs_ref[...], all_ref[...], (((0,), (0,)), ((), ())), preferred_element_type=F32
+            ).astype(BF16)
+            ones = jnp.ones((8, TOKENS), BF16)
+            bias_grad[...] = jnp.dot(ones, all_ref[...], preferred_element_type=F32)
+
     gather_and_pick(
-        at, net, pnet, res, all_ref, w_ref, id_ref, None, parts, back_ref, own.wait, lambda i: None
+        at, net, pnet, res, all_ref, w_ref, id_ref, None, parts, back_ref, own.wait, extra
     )
     for k in range(8):
         mnet.sent(k, mrecv.at[k])
@@ -501,7 +515,7 @@
     ynet.sent(8, far_out)
 
 
-def residuals(pre, ids, w, xs, ws, target, bias):
+def residuals(pre, ids, w, xs, ws, target, bias, base):
     vm = pl.BlockSpec(memory_space=pltpu.VMEM)
     hbm = pl.BlockSpec(memory_space=pl.ANY)
     dma = pltpu.SemaphoreType.DMA
@@ -511,12 +525,13 @@
             jax.ShapeDtypeStruct((ROWS, COLS), BF16),
             jax.ShapeDtypeStruct((TOKENS, COLS), BF16),
             jax.ShapeDtypeStruct((SLOTS, TOKENS), F32),
+            jax.ShapeDtypeStruct((SKIP, COLS), BF16),
+            jax.ShapeDtypeStruct((8, COLS), F32),
         ],
-        in_specs=[vm, vm, hbm, vm, vm, vm, vm],
-        out_specs=[vm, vm, vm],
+        in_specs=[vm, vm, hbm, vm, vm, vm, vm, vm],
+        out_specs=[vm] * 5,
         scratch_shapes=[
             pltpu.VMEM((FEATS, COLS), BF16),
-            pltpu.VMEM((SLAB, FEATS), BF16),
             pltpu.VMEM((PAIR, FEATS), BF16),
             pltpu.VMEM((PAIR, 128), F32),
             pltpu.VMEM((TOKENS, COLS), F32),
@@ -535,15 +550,18 @@
             collective_id=1, has_side_effects=True, vmem_limit_bytes=VMEM_LIMIT
         ),
         name="residuals",
-    )(pre, ids, w, xs, ws, target, bias)
+    )(pre, ids, w, xs, ws, target, bias, base)
 
 
 def grad_kernel(
-    id_ref, pre_ref, back_ref, x_ref, r_ref, ge_ref, gd_ref, st_ref, at_ref, base_ref
+    id_ref, pre_ref, back_ref, base_ref, x_ref, r_ref, ge_ref, gd_ref, gb_ref, st_ref, at_ref
 ):
     feats = base_ref.shape[0]
-    number = pl.program_id(0) * feats + lax.broadcasted_iota(jnp.int32, (feats, 128), 0)
-    base_ref[...] = key_of(number).astype(BF16)
+
+    @pl.when(pl.program_id(0) == 0)
+    def _():
+        gb_ref[...] = bias_grads(id_ref, pre_ref, back_ref)
+
     for t in range(TOKENS // 128):
         lanes = slice(t * 128, (t + 1) * 128)
         pre = pre_ref[:, lanes]
@@ -572,72 +590,50 @@
     gd_ref[...] = jnp.dot(at_ref[...], r_ref[...], preferred_element_type=F32).astype(BF16)
 
 
-def grads(ids, pre, back, x, r, feats=512):
+def grads(ids, pre, back, base, x, r, feats=1024):
     slots = pl.BlockSpec((SLOTS, TOKENS), lambda i: (0, 0))
     whole = pl.BlockSpec((TOKENS, COLS), lambda i: (0, 0))
     out = pl.BlockSpec((feats, COLS), lambda i: (i, 0))
     return pl.pallas_call(
         grad_kernel,
         grid=(FEATS // feats,),
-        in_specs=[slots, slots, slots, whole, whole],
-        out_specs=[out, out],
-        out_shape=[jax.ShapeDtypeStruct((FEATS, COLS), BF16)] * 2,
-        scratch_shapes=[pltpu.VMEM((feats, TOKENS), BF16)] * 2 + [pltpu.VMEM((feats, 128), BF16)],
+        in_specs=[slots, slots, slots, pl.BlockSpec((feats, 128), lambda i: (i, 0)), whole, whole],
+        out_specs=[out, out, pl.BlockSpec((FEATS // 128, 128), lambda i: (0, 0))],
+        out_shape=[jax.ShapeDtypeStruct((FEATS, COLS), BF16)] * 2
+        + [jax.ShapeDtypeStruct((FEATS // 128, 128), F32)],
+        scratch_shapes=[pltpu.VMEM((feats, TOKENS), BF16)] * 2,
         compiler_params=pltpu.CompilerParams(vmem_limit_bytes=VMEM_LIMIT),
         name="grads",
-    )(ids, pre, back, x, r)
-
-
-def small_kernel(id_ref, pre_ref, back_ref, xs_ref, r_ref, gb_ref, gs_ref, bd_ref):
+    )(ids, pre, back, base, x, r)
+
+
+def bias_grads(id_ref, pre_ref, back_ref):
     total = jnp.zeros((FEATS // 128, 128), F32)
-    contract = (((0,), (0,)), ((), ()))
     pairs = (((1,), (1,)), ((), ()))
-    for t in range(TOKENS // 512):
-        lanes = slice(t * 512, (t + 1) * 512)
-        ids = id_ref[:, lanes]
-        high, low = ids >> 7, ids & 127
-        slope = jnp.where(pre_ref[:, lanes] > 0.0, back_ref[:, lanes], 0.0)
-        top = slope.astype(BF16).astype(F32)
-        rest = slope - top
-        rest_top = rest.astype(BF16).astype(F32)
-        last = rest - rest_top
-        lines = lax.broadcasted_iota(jnp.int32, (FEATS // 128, 512), 0)
-        lanes128 = lax.broadcasted_iota(jnp.int32, (128, 512), 0)
-        for j in range(SLOTS):
-            row = slice(j, j + 1)
-            one = jnp.where(high[row, :] == lines, 1.0, 0.0).astype(BF16)
-            hit = low[row, :] == lanes128
-            for value in (top, rest_top, last):
-                table = jnp.where(hit, value[row, :], 0.0).astype(BF16)
-                total += lax.dot_general(one, table, pairs, preferred_element_type=F32)
-    gb_ref[...] = total
-    gs_ref[...] = lax.dot_general(
-        xs_ref[...], r_ref[...], contract, preferred_element_type=F32
-    ).astype(BF16)
-    bd_ref[...] = jnp.dot(jnp.ones((8, TOKENS), BF16), r_ref[...], preferred_element_type=F32)
-
-
-def small_grads(ids, pre, back, xs, r):
-    return pl.pallas_call(
-        small_kernel,
-        in_specs=[pl.BlockSpec(memory_space=pltpu.VMEM)] * 5,
-        out_specs=[pl.BlockSpec(memory_space=pltpu.VMEM)] * 3,
-        out_shape=[
-            jax.ShapeDtypeStruct((FEATS // 128, 128), F32),
-            jax.ShapeDtypeStruct((SKIP, COLS), BF16),
-            jax.ShapeDtypeStruct((8, COLS), F32),
-        ],
-        compiler_params=pltpu.CompilerParams(vmem_limit_bytes=VMEM_LIMIT),
-        name="small_grads",
-    )(ids, pre, back, xs, r)
+    ids = id_ref[...]
+    high, low = ids >> 7, ids & 127
+    slope = jnp.where(pre_ref[...] > 0.0, back_ref[...], 0.0)
+    top = slope.astype(BF16).astype(F32)
+    rest = slope - top
+    lines = lax.broadcasted_iota(jnp.int32, (FEATS // 128, TOKENS), 0)
+    lines128 = lax.broadcasted_iota(jnp.int32, (128, TOKENS), 0)
+    for j in range(SLOTS):
+        row = slice(j, j + 1)
+        one = jnp.where(high[row, :] == lines, 1.0, 0.0).astype(BF16)
+        hit = low[row, :] == lines128
+        for value in (top, rest):
+            table = jnp.where(hit, value[row, :], 0.0).astype(BF16)
+            total += lax.dot_general(one, table, pairs, preferred_element_type=F32)
+    return total
 
 
 def shards(inputs, target, feature_slots, w_enc, b_enc, w_dec, b_dec, w_skip):
     ids = feature_slots[:, 0, :].T
-    all_x, x_skip, pre = encode(inputs, ids, w_enc, b_enc.reshape(FEATS // 128, 128))
-    recon, all_r, back = residuals(pre, ids, w_dec, x_skip, w_skip, target, b_dec[None, :])
-    grad_enc, grad_dec = grads(ids, pre, back, all_x, all_r)
-    grad_benc, grad_skip, grad_bdec = small_grads(ids, pre, back, x_skip, all_r)
+    all_x, x_skip, pre, base_row, base_col = encode(inputs, ids, w_enc, b_enc.reshape(FEATS // 128, 128))
+    recon, all_r, back, grad_skip, grad_bdec = residuals(
+        pre, ids, w_dec, x_skip, w_skip, target, b_dec[None, :], base_row
+    )
+    grad_enc, grad_dec, grad_benc = grads(ids, pre, back, base_col, all_x, all_r)
     return recon, grad_enc, grad_dec, grad_benc.reshape(-1), grad_bdec[0], grad_skip
 
 

time: 169 us -> 155 us (0.917)
  Pallas kernels: 165 us -> 151 us
    pallas_call x1, Pallas kernels: 42.3 us -> 33.4 us  [grads(): pl.pallas_call(grad_kernel, grid=(FEATS // feats,), in_specs=[slots, slot...]
    pallas_call x1 -> x0, Pallas kernels: 7.21 us -> none  [small_grads(): pl.pallas_call(small_kernel, in_specs=[pl.BlockSpec(memory_space=pltpu.VM...]
where the time goes in v3:
time: 155 us; the launch traced here: 154 us
  Pallas kernels  151 us (97%)
  local copies, waits for them, and re-layouts  2.71 us (2%)
    pallas_call x1, Pallas kernels, residuals(): pl.pallas_call(residual_kernel, out_shape=[jax.ShapeDtypeStruct((ROWS, CO...  70.9 us
    pallas_call x1, Pallas kernels, encode(): pl.pallas_call(encode_kernel, out_shape=[jax.ShapeDtypeStruct((TOKENS, CO...  46.3 us
    pallas_call x1, Pallas kernels, grads(): pl.pallas_call(grad_kernel, grid=(FEATS // feats,), in_specs=[slots, slot...  33.4 us

profile of v3, /device:TPU:0, one launch (start us, length us, event | category | flops | bytes accessed | tf_op | source)
XLA Modules:
  0.0 153.9 jit_solution(486109416304595743)
XLA Ops:
  0.6 46.3 %encode.1 = (bf16[2048,512]{1,0:T(8,128)(2,1)}, bf16[2048,256]{1,0:T(8,128)(2,1)}, f32[8,2048]{1,0:T(8,128)}, bf16[32,4096]{1,0:T(8,128)(2,1)}, bf16[4096,128]{1,0:T(8,128)(2,1)}) custom-call(bf16[128,512]{1,0:T(8,128)(2,1)} %x_ref.1, s32[8,2048]{1,0:T(8,128)} %bitcast.7, bf16[4096,512]{1,0:T(8,128)(2,1)} %w_hbm.2, f32[32,128]{1,0:T(8,128)} %bitcast.10), custom_call_target="tpu_custom_call" | custom-call | tf_op jit(solution)/shard_map/encode/pallas_call | solution.py:350
  46.9 70.9 %residuals.1 = (bf16[128,512]{1,0:T(8,128)(2,1)}, bf16[2048,512]{1,0:T(8,128)(2,1)}, f32[8,2048]{1,0:T(8,128)}, bf16[256,512]{1,0:T(8,128)(2,1)}, f32[8,512]{1,0:T(8,128)}) custom-call(f32[8,2048]{1,0:T(8,128)} %get-tuple-element.19.pre_ref, s32[8,2048]{1,0:T(8,128)} %bitcast.8, bf16[4096,512]{1,0:T(8,128)(2,1)} %w_hbm.3, ...), custom_call_target="tpu_custom_call" | custom-call | tf_op jit(solution)/shard_map/residuals/pallas_call | solution.py:522
  117.8 0.0 copy-start.1
  117.8 0.0 copy-start
  117.8 1.3 slice.3
  119.2 33.4 %grads.1 = (bf16[4096,512]{1,0:T(8,128)(2,1)}, bf16[4096,512]{1,0:T(8,128)(2,1)}, f32[32,128]{1,0:T(8,128)}) custom-call(s32[8,2048]{1,0:T(8,128)} %bitcast.9, f32[8,2048]{1,0:T(8,128)} %get-tuple-element.19.pre_ref, f32[8,2048]{1,0:T(8,128)} %get-tuple-element.23.back_ref, bf16[4096,128]{1,0:T(8,128)(2,1)} %get-tuple-element.24.base_ref, ...), custom_call_target="tpu_custom_call" | custom-call | tf_op jit(solution)/shard_map/grads/pallas_call | solution.py:597
  152.6 0.0 copy-done.1
  152.6 0.7 copy.16
  153.2 0.0 copy-done
  153.2 0.7 copy.17
Async XLA Ops:
  117.8 34.8 %copy-start.1 = (bf16[128,512]{1,0:T(8,128)(2,1)S(1)}, bf16[128,512]{1,0:T(8,128)(2,1)}, u32[]{:S(2)}) copy-start(bf16[128,512]{1,0:T(8,128)(2,1)} %get-tuple-element.38) | copy-start | bytes 393220
  117.8 35.4 %copy-start = (bf16[256,512]{1,0:T(8,128)(2,1)S(1)}, bf16[256,512]{1,0:T(8,128)(2,1)}, u32[]{:S(2)}) copy-start(bf16[256,512]{1,0:T(8,128)(2,1)} %get-tuple-element.43) | copy-start | bytes 786436

commit v4 on v3

--- a/solution.py
+++ b/solution.py
@@ -115,11 +115,22 @@
             dots = dots + jnp.concatenate([bias[lines, :]] * 2, axis=1)
         for j in range(SLOTS):
             row = ids[j : j + 1, :]
-            tree = dots
-            for bit in range(4, -1, -1):
-                half = tree.shape[0] // 2
-                upper = jnp.broadcast_to((row & (8 << bit)) != 0, (half, PAIR))
-                tree = jnp.where(upper, tree[half:], tree[:half])
+
+            def narrow(tree, down_to):
+                while tree.shape[0] > down_to:
+                    half = tree.shape[0] // 2
+                    upper = jnp.broadcast_to((row & half) != 0, (half, PAIR))
+                    tree = jnp.where(upper, tree[half:], tree[:half])
+                return tree
+
+            blocks = [narrow(dots[64 * i : 64 * (i + 1)], 8) for i in range(width // 64)]
+            tree = blocks
+            bit = 64
+            while len(tree) > 1:
+                upper = jnp.broadcast_to((row & bit) != 0, (8, PAIR))
+                tree = [jnp.where(upper, b, a) for a, b in zip(tree[::2], tree[1::2])]
+                bit *= 2
+            tree = tree[0]
             here = jnp.broadcast_to((row >> 8) == c, (8, PAIR))
             accs[j] = jnp.where(here, tree, accs[j])
     line = lax.broadcasted_iota(jnp.int32, (8, PAIR), 0)
@@ -130,7 +141,7 @@
     return jnp.concatenate(out, axis=0)
 
 
-def gather_and_pick(at, net, pnet, own, rows_ref, w_ref, id_ref, bias, parts, out_ref, keep, extra):
+def gather_and_pick(at, net, pnet, own, rows_ref, w_ref, id_ref, bias, parts, keep, extra):
     def blk(b, dy, half=None, other=False):
         return rows_ref.at[seq_rows(at.seq(b, dy, other), half)]
 
@@ -186,36 +197,34 @@
             net.wait(18, blk(1, 2, 1, True))
         extra(i)
 
-    def pair_of(k):
-        return choose(k, [lax.div(at.seq(b, dy), 2) for b, dy in PICK_ORDER])
-
-    def lanes(k):
-        return pl.ds(pl.multiple_of(pair_of(k) * PAIR, PAIR), PAIR)
-
     def body(k, carry):
         for i in range(1, 8):
             pl.when(k == i)(functools.partial(step, i))
-        q = pair_of(k)
-        rows = rows_ref[pl.ds(pl.multiple_of(q * PAIR, PAIR), PAIR), :]
-        parts[k, at.p] = pick_slots(rows, w_ref, id_ref[:, lanes(k)], bias)
+        span = pair_lanes(at, PICK_ORDER, k)
+        parts[k, at.p] = pick_slots(rows_ref[span, :], w_ref, id_ref[:, span], bias)
         for d in range(1, N_TP):
             here = parts.at[k, at.p]
             pnet.start((k, d), here, here, (at.s, lax.rem(at.p + d, N_TP)))
         return carry
 
     lax.fori_loop(0, 8, body, 0)
-    extra(8)
-
-    def add_up(k, carry):
-        for d in range(1, N_TP):
-            pnet.wait((k, d), parts.at[k, lax.rem(at.p + N_TP - d, N_TP)])
-        total = parts[k, 0]
-        for q in range(1, N_TP):
-            total = total + parts[k, q]
-        out_ref[:, lanes(k)] = total
-        return carry
-
-    lax.fori_loop(0, 8, add_up, 0)
+
+
+def pair_lanes(at, order, k):
+    q = choose(k, [lax.div(at.seq(b, dy), 2) for b, dy in order])
+    return pl.ds(pl.multiple_of(q * PAIR, PAIR), PAIR)
+
+
+def add_up(at, pnet, parts, out_ref, k):
+    for d in range(1, N_TP):
+        pnet.wait((k, d), parts.at[k, lax.rem(at.p + N_TP - d, N_TP)])
+    total = parts[k, 0]
+    for q in range(1, N_TP):
+        total = total + parts[k, q]
+    out_ref[:, pair_lanes(at, PICK_ORDER, k)] = total
+
+
+def all_sent(at, net, pnet, rows_ref, parts):
     for i in range(SEQ_KINDS):
         net.sent(i, rows_ref.at[pl.ds(0, ROWS // 2 if i in HALVES else ROWS)])
 
@@ -227,16 +236,34 @@
     lax.fori_loop(0, 8, done, 0)
 
 
-def encode_kernel(
-    x_ref, id_ref, w_hbm, b_ref, all_ref, skip_ref, pre_ref, base_row, base_col, w_ref, bias, parts,
-    send, recv, psend, precv, send2, recv2, local,
+SUM_ORDER = ((0, 2), (1, 2), (1, 1), (1, 3), (1, 0), (0, 1), (0, 3), (0, 0))
+SLAB = 32
+
+
+class Sender2(Sender):
+    def copy(self, i, src, dst, dev):
+        return pltpu.make_async_remote_copy(
+            src_ref=src, dst_ref=dst, send_sem=self.send.at[i[0], i[1]],
+            recv_sem=self.recv.at[i[0], i[1]], device_id=dev, device_id_type=MESH,
+        )
+
+
+def step_kernel(
+    x_ref, id_ref, we_hbm, b_ref, wd_hbm, ws_ref, target, dec_bias,
+    recon, x_hbm, r_hbm, pre_ref, back_ref, col_hbm, skip_grad, bias_grad,
+    we_ref, wd_ref, all_ref, res_ref, skip_ref, base_row, base_col, bias, enc_parts, back_parts,
+    table, turned, part, mrecv, out_buf, half_in, full_in, far_out, far_in, res,
+    send, recv, psend, precv, send2, recv2, msend, mrcv, ysend, yrcv, send3, recv3, psend3, precv3,
+    local,
 ):
     at = Place()
     here = (at.s, at.p)
-    load = pltpu.make_async_copy(w_hbm, w_ref, local.at[0])
+    load = pltpu.make_async_copy(we_hbm, we_ref, local.at[0])
     load.start()
     own = pltpu.make_async_copy(x_ref, all_ref.at[seq_rows(at.s)], local.at[1])
     own.start()
+    load_dec = pltpu.make_async_copy(wd_hbm, wd_ref, local.at[3])
+    load_dec.start()
 
     half_p = lax.div(at.s, 2)
     stay = half_p == at.p
@@ -263,11 +290,11 @@
 
     net, pnet, net2 = Sender(send, recv, here), Sender2(psend, precv, here), Sender(send2, recv2, here)
 
-    def part(h):
+    def columns(h):
         return x_ref.at[:, pl.ds(pl.multiple_of(h * SKIP, SKIP), SKIP)]
 
     land = skip_ref.at[seq_rows(at.s)]
-    inside = pltpu.make_async_copy(part(at.c), land, local.at[2])
+    inside = pltpu.make_async_copy(columns(at.c), land, local.at[2])
 
     def piece(b, dx, half=None):
         q = at.tp(b, dx)
@@ -284,11 +311,11 @@
 
     def extra(i):
         if i == 0:
-            net2.start(1, part(1 - at.c), land, cross)
+            net2.start(1, columns(1 - at.c), land, cross)
 
             @pl.when(jnp.logical_not(stay))
             def _():
-                net2.start(0, part(at.c), land, same)
+                net2.start(0, columns(at.c), land, same)
 
             @pl.when(stay)
             def _():
@@ -303,7 +330,7 @@
 
             @pl.when(stay)
             def _():
-                pltpu.make_async_copy(part(at.c), land, local.at[2]).wait()
+                pltpu.make_async_copy(columns(at.c), land, local.at[2]).wait()
 
             net2.start(10, piece(0, 0), piece(0, 0), at.side)
             net2.start(2, piece(0, 0), piece(0, 0), at.right)
@@ -324,74 +351,13 @@
         load.wait()
         own.wait()
 
-    gather_and_pick(at, net, pnet, x_ref, all_ref, w_ref, id_ref, bias, parts, pre_ref, keep, extra)
-
-    @pl.when(jnp.logical_not(stay))
-    def _():
-        net2.sent(0, land)
-
-    net2.sent(1, land)
-    for i in range(2, 11):
-        net2.sent(i, skip_ref.at[pl.ds(0, 128 if i in (4, 5, 8, 9) else 256)])
-
-
-class Sender2(Sender):
-    def copy(self, i, src, dst, dev):
-        return pltpu.make_async_remote_copy(
-            src_ref=src, dst_ref=dst, send_sem=self.send.at[i[0], i[1]],
-            recv_sem=self.recv.at[i[0], i[1]], device_id=dev, device_id_type=MESH,
-        )
-
-
-def encode(x, ids, w, bias):
-    vm = pl.BlockSpec(memory_space=pltpu.VMEM)
-    hbm = pl.BlockSpec(memory_space=pl.ANY)
-    dma = pltpu.SemaphoreType.DMA
-    return pl.pallas_call(
-        encode_kernel,
-        out_shape=[
-            jax.ShapeDtypeStruct((TOKENS, COLS), BF16),
-            jax.ShapeDtypeStruct((TOKENS, SKIP), BF16),
-            jax.ShapeDtypeStruct((SLOTS, TOKENS), F32),
-            jax.ShapeDtypeStruct((SLAB, FEATS), BF16),
-            jax.ShapeDtypeStruct((FEATS, 128), BF16),
-        ],
-        in_specs=[hbm, vm, hbm, vm],
-        out_specs=[vm] * 5,
-        scratch_shapes=[
-            pltpu.VMEM((FEATS, COLS), BF16),
-            pltpu.VMEM((FEATS, 128), F32),
-            pltpu.VMEM((8, N_TP, SLOTS, PAIR), F32),
-            dma((SEQ_KINDS,)), dma((SEQ_KINDS,)), dma((8, N_TP)), dma((8, N_TP)),
-            dma((11,)), dma((11,)), dma((3,)),
-        ],
-        compiler_params=pltpu.CompilerParams(
-            collective_id=0, has_side_effects=True, vmem_limit_bytes=VMEM_LIMIT
-        ),
-        name="encode",
-    )(x, ids, w, bias)
-
-
-SUM_ORDER = tuple((b, dy) for b in (1, 0) for dy in (2, 1, 3, 0))
-SLAB = 32
-
-
-def residual_kernel(
-    pre_ref, id_ref, w_hbm, xs_ref, ws_ref, target, bias, base, recon, all_ref, back_ref, skip_grad,
-    bias_grad, w_ref, table, turned, part, mrecv, out_buf, half_in, full_in, far_out, far_in, res, parts,
-    msend, mrcv, ysend, yrcv, send, recv, psend, precv, local,
-):
-    at = Place()
-    here = (at.s, at.p)
-    load = pltpu.make_async_copy(w_hbm, w_ref, local.at[0])
-    load.start()
-    peers = [(at.s, lax.rem(at.p + d, N_TP)) for d in range(1, N_TP)]
-    around = [at.mate, at.up, at.down, at.far] + peers
-    barrier = pltpu.get_barrier_semaphore()
-    for dev in around:
-        pl.semaphore_signal(barrier, inc=1, device_id=dev, device_id_type=MESH)
-    pl.semaphore_wait(barrier, len(around))
-    load.wait()
+    gather_and_pick(at, net, pnet, x_ref, all_ref, we_ref, id_ref, bias, enc_parts, keep, extra)
+    extra(8)
+    out_x = pltpu.make_async_copy(all_ref, x_hbm, local.at[4])
+    out_x.start()
+    out_col = pltpu.make_async_copy(base_col, col_hbm, local.at[5])
+    out_col.start()
+    load_dec.wait()
 
     mnet, ynet = Sender(msend, mrcv, here), Sender(ysend, yrcv, here)
     H = ROWS // 2
@@ -403,13 +369,14 @@
         return part[rows, :] + mrecv[k, mine, :]
 
     def opposite(i):
-        mnet.wait(4 * i, mrecv.at[4 * i])
-        out_buf[3 * i] = pair(4 * i).astype(BF16)
+        k = SUM_ORDER.index((1 - i, 2))
+        mnet.wait(k, mrecv.at[k])
+        out_buf[3 * i] = pair(k).astype(BF16)
         ynet.start(4 * i, out_buf.at[3 * i, pl.ds(0, H)], half_in.at[2 * i], at.up)
         ynet.start(4 * i + 1, out_buf.at[3 * i, pl.ds(H, H)], half_in.at[2 * i + 1], at.down)
 
     def upward(i):
-        k = 4 * i + 1
+        k = SUM_ORDER.index((1 - i, 1))
         mnet.wait(k, mrecv.at[k])
         out_buf[3 * i + 1, H:, :] = pair(k, 1).astype(BF16)
         ynet.wait(4 * i, half_in.at[2 * i])
@@ -417,7 +384,7 @@
         ynet.start(4 * i + 2, out_buf.at[3 * i + 1], full_in.at[2 * i], at.up)
 
     def downward(i):
-        k = 4 * i + 2
+        k = SUM_ORDER.index((1 - i, 3))
         mnet.wait(k, mrecv.at[k])
         out_buf[3 * i + 2, :H, :] = pair(k, 0).astype(BF16)
         ynet.wait(4 * i + 1, half_in.at[2 * i + 1])
@@ -425,7 +392,7 @@
         ynet.start(4 * i + 3, out_buf.at[3 * i + 2], full_in.at[2 * i + 1], at.down)
 
     def here_sum(i):
-        k = 4 * i + 3
+        k = SUM_ORDER.index((1 - i, 0))
         mnet.wait(k, mrecv.at[k])
         ynet.wait(4 * i + 2, full_in.at[2 * i])
         ynet.wait(4 * i + 3, full_in.at[2 * i + 1])
@@ -433,16 +400,16 @@
 
     def step(i):
         if i == 1:
+            opposite(1)
+        if i == 2:
             opposite(0)
-        if i == 2:
+        if i == 3:
             upward(0)
-        if i == 3:
+        if i == 4:
             downward(0)
-        if i == 5:
-            opposite(1)
+        if i == 6:
             far_out[...] = here_sum(0)
             ynet.start(8, far_out, far_in, at.far)
-        if i == 6:
             upward(1)
         if i == 7:
             downward(1)
@@ -450,6 +417,7 @@
     filler = jnp.zeros((128 - 2 * SLOTS, 128), F32)
 
     def body(k, carry):
+        add_up(at, pnet, enc_parts, pre_ref, choose(k, [PICK_ORDER.index(o) for o in SUM_ORDER]))
         q = choose(k, [lax.div(at.seq(b, dy), 2) for b, dy in SUM_ORDER])
         first = pl.multiple_of(q * PAIR, PAIR)
         for t in range(2):
@@ -467,7 +435,7 @@
                 keys.append(jnp.broadcast_to(both[:, SLOTS + j : SLOTS + j + 1], (SLAB, 128)).astype(BF16))
                 vals.append(jnp.broadcast_to(both[:, j : j + 1], (SLAB, 128)).astype(BF16))
             for g in range(FEATS // 128):
-                spot = base[:, g * 128 : (g + 1) * 128]
+                spot = base_row[:, g * 128 : (g + 1) * 128]
                 acc = jnp.zeros((SLAB, 128), BF16)
                 for j in range(SLOTS):
                     acc = jnp.where(keys[j] == spot, vals[j], acc)
@@ -476,8 +444,8 @@
 
         lax.fori_loop(0, PAIR // SLAB, slab, 0)
         rows = pl.ds(first, PAIR)
-        part[rows, :] = jnp.dot(table[...], w_ref[...], preferred_element_type=F32) + jnp.dot(
-            xs_ref[rows, :], ws_ref[...], preferred_element_type=F32
+        part[rows, :] = jnp.dot(table[...], wd_ref[...], preferred_element_type=F32) + jnp.dot(
+            skip_ref[rows, :], ws_ref[...], preferred_element_type=F32
         )
         mnet.start(k, part.at[seq_rows(2 * q + 1 - at.c)], mrecv.at[k], at.mate)
         for i in range(1, 8):
@@ -485,26 +453,40 @@
         return carry
 
     lax.fori_loop(0, 8, body, 0)
-    total = here_sum(1) + bias[...]
+    total = here_sum(1) + dec_bias[...]
     ynet.wait(8, far_in)
     total = total + far_in[...]
     recon[...] = total.astype(BF16)
     res[...] = (total - target[...].astype(F32)).astype(BF16)
-    own = pltpu.make_async_copy(res, all_ref.at[seq_rows(at.s)], local.at[1])
+    own = pltpu.make_async_copy(res, res_ref.at[seq_rows(at.s)], local.at[6])
     own.start()
-    net, pnet = Sender(send, recv, here), Sender2(psend, precv, here)
-
-    def extra(i):
-        if i == 8:
-            skip_grad[...] = lax.dot_general(
-                xs_ref[...], all_ref[...], (((0,), (0,)), ((), ())), preferred_element_type=F32
-            ).astype(BF16)
-            ones = jnp.ones((8, TOKENS), BF16)
-            bias_grad[...] = jnp.dot(ones, all_ref[...], preferred_element_type=F32)
-
+    net3, pnet3 = Sender(send3, recv3, here), Sender2(psend3, precv3, here)
     gather_and_pick(
-        at, net, pnet, res, all_ref, w_ref, id_ref, None, parts, back_ref, own.wait, extra
+        at, net3, pnet3, res, res_ref, wd_ref, id_ref, None, back_parts, own.wait, lambda i: None
     )
+    out_r = pltpu.make_async_copy(res_ref, r_hbm, local.at[7])
+    out_r.start()
+    skip_grad[...] = lax.dot_general(
+        skip_ref[...], res_ref[...], (((0,), (0,)), ((), ())), preferred_element_type=F32
+    ).astype(BF16)
+    ones = jnp.ones((8, TOKENS), BF16)
+    bias_grad[...] = jnp.dot(ones, res_ref[...], preferred_element_type=F32)[:1]
+
+    def add_back(k, carry):
+        add_up(at, pnet3, back_parts, back_ref, k)
+        return carry
+
+    lax.fori_loop(0, 8, add_back, 0)
+    all_sent(at, net, pnet, all_ref, enc_parts)
+    all_sent(at, net3, pnet3, res_ref, back_parts)
+
+    @pl.when(jnp.logical_not(stay))
+    def _():
+        net2.sent(0, land)
+
+    net2.sent(1, land)
+    for i in range(2, 11):
+        net2.sent(i, skip_ref.at[pl.ds(0, 128 if i in (4, 5, 8, 9) else 256)])
     for k in range(8):
         mnet.sent(k, mrecv.at[k])
     for i in (0, 1):
@@ -513,25 +495,40 @@
         ynet.sent(4 * i + 2, full_in.at[0])
         ynet.sent(4 * i + 3, full_in.at[0])
     ynet.sent(8, far_out)
-
-
-def residuals(pre, ids, w, xs, ws, target, bias, base):
+    out_x.wait()
+    out_col.wait()
+    out_r.wait()
+
+
+def step(x, ids, w_enc, b_enc, w_dec, w_skip, target, b_dec):
     vm = pl.BlockSpec(memory_space=pltpu.VMEM)
     hbm = pl.BlockSpec(memory_space=pl.ANY)
     dma = pltpu.SemaphoreType.DMA
     return pl.pallas_call(
-        residual_kernel,
+        step_kernel,
         out_shape=[
             jax.ShapeDtypeStruct((ROWS, COLS), BF16),
             jax.ShapeDtypeStruct((TOKENS, COLS), BF16),
+            jax.ShapeDtypeStruct((TOKENS, COLS), BF16),
             jax.ShapeDtypeStruct((SLOTS, TOKENS), F32),
+            jax.ShapeDtypeStruct((SLOTS, TOKENS), F32),
+            jax.ShapeDtypeStruct((FEATS, 128), BF16),
             jax.ShapeDtypeStruct((SKIP, COLS), BF16),
-            jax.ShapeDtypeStruct((8, COLS), F32),
+            jax.ShapeDtypeStruct((1, COLS), F32),
         ],
-        in_specs=[vm, vm, hbm, vm, vm, vm, vm, vm],
-        out_specs=[vm] * 5,
+        in_specs=[hbm, vm, hbm, vm, hbm, vm, vm, vm],
+        out_specs=[vm, hbm, hbm, vm, vm, hbm, vm, vm],
         scratch_shapes=[
             pltpu.VMEM((FEATS, COLS), BF16),
+            pltpu.VMEM((FEATS, COLS), BF16),
+            pltpu.VMEM((TOKENS, COLS), BF16),
+            pltpu.VMEM((TOKENS, COLS), BF16),
+            pltpu.VMEM((TOKENS, SKIP), BF16),
+            pltpu.VMEM((SLAB, FEATS), BF16),
+            pltpu.VMEM((FEATS, 128), BF16),
+            pltpu.VMEM((FEATS, 128), F32),
+            pltpu.VMEM((8, N_TP, SLOTS, PAIR), F32),
+            pltpu.VMEM((8, N_TP, SLOTS, PAIR), F32),
             pltpu.VMEM((PAIR, FEATS), BF16),
             pltpu.VMEM((PAIR, 128), F32),
             pltpu.VMEM((TOKENS, COLS), F32),
@@ -542,15 +539,15 @@
             pltpu.VMEM((ROWS, COLS), F32),
             pltpu.VMEM((ROWS, COLS), F32),
             pltpu.VMEM((ROWS, COLS), BF16),
-            pltpu.VMEM((8, N_TP, SLOTS, PAIR), F32),
-            dma((8,)), dma((8,)), dma((9,)), dma((9,)),
-            dma((SEQ_KINDS,)), dma((SEQ_KINDS,)), dma((8, N_TP)), dma((8, N_TP)), dma((2,)),
+            dma((SEQ_KINDS,)), dma((SEQ_KINDS,)), dma((8, N_TP)), dma((8, N_TP)),
+            dma((11,)), dma((11,)), dma((8,)), dma((8,)), dma((9,)), dma((9,)),
+            dma((SEQ_KINDS,)), dma((SEQ_KINDS,)), dma((8, N_TP)), dma((8, N_TP)), dma((8,)),
         ],
         compiler_params=pltpu.CompilerParams(
-            collective_id=1, has_side_effects=True, vmem_limit_bytes=VMEM_LIMIT
+            collective_id=0, has_side_effects=True, vmem_limit_bytes=VMEM_LIMIT
         ),
-        name="residuals",
-    )(pre, ids, w, xs, ws, target, bias, base)
+        name="step",
+    )(x, ids, w_enc, b_enc, w_dec, w_skip, target, b_dec)
 
 
 def grad_kernel(
@@ -629,12 +626,11 @@
 
 def shards(inputs, target, feature_slots, w_enc, b_enc, w_dec, b_dec, w_skip):
     ids = feature_slots[:, 0, :].T
-    all_x, x_skip, pre, base_row, base_col = encode(inputs, ids, w_enc, b_enc.reshape(FEATS // 128, 128))
-    recon, all_r, back, grad_skip, grad_bdec = residuals(
-        pre, ids, w_dec, x_skip, w_skip, target, b_dec[None, :], base_row
+    recon, all_x, all_r, pre, back, base, grad_skip, grad_bdec = step(
+        inputs, ids, w_enc, b_enc.reshape(FEATS // 128, 128), w_dec, w_skip, target, b_dec[None, :]
     )
-    grad_enc, grad_dec, grad_benc = grads(ids, pre, back, base_col, all_x, all_r)
-    return recon, grad_enc, grad_dec, grad_benc.reshape(-1), grad_bdec[0], grad_skip
+    grad_enc, grad_dec, grad_benc = grads(ids, pre, back, base, all_x, all_r)
+    return recon, grad_enc, grad_dec, grad_benc.reshape(-1), grad_bdec.reshape(-1), grad_skip
 
 
 def solution(mesh):

time: 155 us -> 142 us (0.916)
  Pallas kernels: 151 us -> 138 us
    pallas_call x2 -> x1, Pallas kernels: 117 us -> 104 us  [step(): pl.pallas_call(step_kernel, out_shape=[jax.ShapeDtypeStruct((ROWS, COLS),...]
where the time goes in v4:
time: 142 us; the launch traced here: 140 us
  Pallas kernels  138 us (97%)
  local copies, waits for them, and re-layouts  1.95 us (1%)
    pallas_call x1, Pallas kernels, step(): pl.pallas_call(step_kernel, out_shape=[jax.ShapeDtypeStruct((ROWS, COLS),...  104 us
    pallas_call x1, Pallas kernels, grads(): pl.pallas_call(grad_kernel, grid=(FEATS // feats,), in_specs=[slots, slot...  33.6 us

profile of v4, /device:TPU:0, one launch (start us, length us, event | category | flops | bytes accessed | tf_op | source)
XLA Modules:
  0.0 140.4 jit_solution(17181180246879077854)
XLA Ops:
  0.6 104.2 %step.1 = (bf16[128,512]{1,0:T(8,128)(2,1)}, bf16[2048,512]{1,0:T(8,128)(2,1)}, bf16[2048,512]{1,0:T(8,128)(2,1)}, f32[8,2048]{1,0:T(8,128)}, f32[8,2048]{1,0:T(...) custom-call(bf16[128,512]{1,0:T(8,128)(2,1)} %x_ref.1, s32[8,2048]{1,0:T(8,128)} %bitcast.7, ...), custom_call_target="tpu_custom_call" | custom-call | tf_op jit(solution)/shard_map/step/pallas_call | solution.py:507
  104.8 0.0 copy-start.1
  104.8 0.0 copy-start.2
  104.8 0.0 copy-start
  104.8 33.6 %grads.1 = (bf16[4096,512]{1,0:T(8,128)(2,1)}, bf16[4096,512]{1,0:T(8,128)(2,1)}, f32[32,128]{1,0:T(8,128)}) custom-call(s32[8,2048]{1,0:T(8,128)} %bitcast.8, f32[8,2048]{1,0:T(8,128)} %get-tuple-element.18.pre_ref, f32[8,2048]{1,0:T(8,128)} %get-tuple-element.19.back_ref, bf16[4096,128]{1,0:T(8,128)(2,1)} %get-tuple-element.20.base_ref, ...), custom_call_target="tpu_custom_call" | custom-call | tf_op jit(solution)/shard_map/grads/pallas_call | solution.py:594
  138.4 0.0 copy-done.1
  138.4 0.7 copy.17
  139.1 0.0 copy-done.2
  139.1 0.6 copy.18
  139.7 0.0 copy-done
  139.7 0.7 copy.19
Async XLA Ops:
  104.8 33.6 %copy-start.1 = (bf16[128,512]{1,0:T(8,128)(2,1)S(1)}, bf16[128,512]{1,0:T(8,128)(2,1)}, u32[]{:S(2)}) copy-start(bf16[128,512]{1,0:T(8,128)(2,1)} %get-tuple-element.34) | copy-start | bytes 393220
  104.8 34.3 %copy-start.2 = (f32[1,512]{1,0:T(1,128)S(1)}, f32[1,512]{1,0:T(1,128)}, u32[]{:S(2)}) copy-start(f32[1,512]{1,0:T(1,128)} %get-tuple-element.26) | copy-start | bytes 6148
  104.8 34.8 %copy-start = (bf16[256,512]{1,0:T(8,128)(2,1)S(1)}, bf16[256,512]{1,0:T(8,128)(2,1)}, u32[]{:S(2)}) copy-start(bf16[256,512]{1,0:T(8,128)(2,1)} %get-tuple-element.39) | copy-start | bytes 786436

commit v5 on v4

--- a/solution.py
+++ b/solution.py
@@ -98,7 +98,16 @@
 
 
 PAIR = 2 * ROWS
-PICK_ORDER = ((0, 0), (0, 3), (0, 1), (1, 0), (0, 2), (1, 3), (1, 1), (1, 2))
+PICK_ORDER = (
+    ((0, 0, False), (0, 0, True)),
+    ((0, 3, False), (0, 1, False)),
+    ((0, 3, True), (0, 1, True)),
+    ((1, 0, False), (1, 0, True)),
+    ((0, 2, False), (0, 2, True)),
+    ((1, 3, False), (1, 1, False)),
+    ((1, 3, True), (1, 1, True)),
+    ((1, 2, False), (1, 2, True)),
+)
 SEQ_KINDS = 19
 HALVES = (2, 3, 6, 7, 12, 13, 17, 18)
 
@@ -173,24 +182,23 @@
     def step(i):
         if i == 1:
             ring(0)
+        if i == 2:
             net.wait(8, blk(1, 0))
             net.start(4, blk(1, 0), blk(1, 0), at.up)
             net.start(5, blk(1, 0), blk(1, 0), at.down)
             net.start(14, blk(1, 0), blk(1, 0), at.mate)
             net.wait(10, blk(0, 3, None, True))
-        if i == 2:
             net.wait(11, blk(0, 1, None, True))
         if i == 3:
-            ring(1)
             last(0)
             net.wait(14, blk(1, 0, None, True))
         if i == 4:
+            ring(1)
             net.wait(12, blk(0, 2, 0, True))
             net.wait(13, blk(0, 2, 1, True))
-        if i == 5:
+        if i == 6:
             last(1)
             net.wait(15, blk(1, 3, None, True))
-        if i == 6:
             net.wait(16, blk(1, 1, None, True))
         if i == 7:
             net.wait(17, blk(1, 2, 0, True))
@@ -200,8 +208,10 @@
     def body(k, carry):
         for i in range(1, 8):
             pl.when(k == i)(functools.partial(step, i))
-        span = pair_lanes(at, PICK_ORDER, k)
-        parts[k, at.p] = pick_slots(rows_ref[span, :], w_ref, id_ref[:, span], bias)
+        one, two = blocks_of(at, k)
+        rows = jnp.concatenate([rows_ref[one, :], rows_ref[two, :]], axis=0)
+        ids = jnp.concatenate([id_ref[:, one], id_ref[:, two]], axis=1)
+        parts[k, at.p] = pick_slots(rows, w_ref, ids, bias)
         for d in range(1, N_TP):
             here = parts.at[k, at.p]
             pnet.start((k, d), here, here, (at.s, lax.rem(at.p + d, N_TP)))
@@ -210,9 +220,8 @@
     lax.fori_loop(0, 8, body, 0)
 
 
-def pair_lanes(at, order, k):
-    q = choose(k, [lax.div(at.seq(b, dy), 2) for b, dy in order])
-    return pl.ds(pl.multiple_of(q * PAIR, PAIR), PAIR)
+def blocks_of(at, k):
+    return [seq_rows(choose(k, [at.seq(*both[i]) for both in PICK_ORDER])) for i in (0, 1)]
 
 
 def add_up(at, pnet, parts, out_ref, k):
@@ -221,7 +230,9 @@
     total = parts[k, 0]
     for q in range(1, N_TP):
         total = total + parts[k, q]
-    out_ref[:, pair_lanes(at, PICK_ORDER, k)] = total
+    one, two = blocks_of(at, k)
+    out_ref[:, one] = total[:, :ROWS]
+    out_ref[:, two] = total[:, ROWS:]
 
 
 def all_sent(at, net, pnet, rows_ref, parts):
@@ -237,6 +248,7 @@
 
 
 SUM_ORDER = ((0, 2), (1, 2), (1, 1), (1, 3), (1, 0), (0, 1), (0, 3), (0, 0))
+NEEDED = (4, 7, 5, 3, 1, 2, 0)
 SLAB = 32
 
 
@@ -321,7 +333,7 @@
             def _():
                 inside.start()
 
-        if i == 2:
+        if i == 1:
             net2.wait(1, skip_ref.at[seq_rows(2 * at.p + 1 - at.c)])
 
             @pl.when(jnp.logical_not(stay))
@@ -335,12 +347,12 @@
             net2.start(10, piece(0, 0), piece(0, 0), at.side)
             net2.start(2, piece(0, 0), piece(0, 0), at.right)
             net2.start(3, piece(0, 0), piece(0, 0), at.left)
-        if i == 4:
+        if i == 3:
             net2.wait(10, piece(1, 0))
             net2.start(6, piece(1, 0), piece(1, 0), at.right)
             net2.start(7, piece(1, 0), piece(1, 0), at.left)
             ring(0)
-        if i == 6:
+        if i == 5:
             ring(1)
         if i == 8:
             for b in (0, 1):
@@ -417,7 +429,15 @@
     filler = jnp.zeros((128 - 2 * SLOTS, 128), F32)
 
     def body(k, carry):
-        add_up(at, pnet, enc_parts, pre_ref, choose(k, [PICK_ORDER.index(o) for o in SUM_ORDER]))
+
+        @pl.when(k < 7)
+        def _():
+            add_up(at, pnet, enc_parts, pre_ref, choose(k, NEEDED))
+
+        @pl.when(k == 2)
+        def _():
+            add_up(at, pnet, enc_parts, pre_ref, 6)
+
         q = choose(k, [lax.div(at.seq(b, dy), 2) for b, dy in SUM_ORDER])
         first = pl.multiple_of(q * PAIR, PAIR)
         for t in range(2):
@@ -443,13 +463,13 @@
             return carry2
 
         lax.fori_loop(0, PAIR // SLAB, slab, 0)
+        for i in range(1, 8):
+            pl.when(k == i)(functools.partial(step, i))
         rows = pl.ds(first, PAIR)
         part[rows, :] = jnp.dot(table[...], wd_ref[...], preferred_element_type=F32) + jnp.dot(
             skip_ref[rows, :], ws_ref[...], preferred_element_type=F32
         )
         mnet.start(k, part.at[seq_rows(2 * q + 1 - at.c)], mrecv.at[k], at.mate)
-        for i in range(1, 8):
-            pl.when(k == i)(functools.partial(step, i))
         return carry
 
     lax.fori_loop(0, 8, body, 0)
@@ -605,7 +625,7 @@
 
 
 def bias_grads(id_ref, pre_ref, back_ref):
-    total = jnp.zeros((FEATS // 128, 128), F32)
+    total = jnp.zeros((FEATS // 128, 256), F32)
     pairs = (((1,), (1,)), ((), ()))
     ids = id_ref[...]
     high, low = ids >> 7, ids & 127
@@ -618,10 +638,10 @@
         row = slice(j, j + 1)
         one = jnp.where(high[row, :] == lines, 1.0, 0.0).astype(BF16)
         hit = low[row, :] == lines128
-        for value in (top, rest):
-            table = jnp.where(hit, value[row, :], 0.0).astype(BF16)
-            total += lax.dot_general(one, table, pairs, preferred_element_type=F32)
-    return total
+        table = [jnp.where(hit, value[row, :], 0.0).astype(BF16) for value in (top, rest)]
+        table = jnp.concatenate(table, axis=0)
+        total += lax.dot_general(one, table, pairs, preferred_element_type=F32)
+    return total[:, :128] + total[:, 128:]
 
 
 def shards(inputs, target, feature_slots, w_enc, b_enc, w_dec, b_dec, w_skip):

time: 142 us -> 137 us (0.965); the launches traced: 140 us -> 137 us
  Pallas kernels: 138 us -> 135 us
    pallas_call x1, Pallas kernels: 104 us -> 101 us  [step(): pl.pallas_call(step_kernel, out_shape=[jax.ShapeDtypeStruct((ROWS, COLS),...]
where the time goes in v5:
time: 137 us
  Pallas kernels  135 us (99%)
  local copies, waits for them, and re-layouts  1.95 us (1%)
    pallas_call x1, Pallas kernels, step(): pl.pallas_call(step_kernel, out_shape=[jax.ShapeDtypeStruct((ROWS, COLS),...  101 us
    pallas_call x1, Pallas kernels, grads(): pl.pallas_call(grad_kernel, grid=(FEATS // feats,), in_specs=[slots, slot...  33.4 us

profile of v5, /device:TPU:0, one launch (start us, length us, event | category | flops | bytes accessed | tf_op | source)
XLA Modules:
  0.0 137.4 jit_solution(3656919355980494419)
XLA Ops:
  0.6 101.4 %step.1 = (bf16[128,512]{1,0:T(8,128)(2,1)}, bf16[2048,512]{1,0:T(8,128)(2,1)}, bf16[2048,512]{1,0:T(8,128)(2,1)}, f32[8,2048]{1,0:T(8,128)}, f32[8,2048]{1,0:T(...) custom-call(bf16[128,512]{1,0:T(8,128)(2,1)} %x_ref.1, s32[8,2048]{1,0:T(8,128)} %bitcast.7, ...), custom_call_target="tpu_custom_call" | custom-call | tf_op jit(solution)/shard_map/step/pallas_call | solution.py:527
  102.0 0.0 copy-start.1
  102.0 0.0 copy-start.2
  102.0 0.0 copy-start
  102.1 33.4 %grads.1 = (bf16[4096,512]{1,0:T(8,128)(2,1)}, bf16[4096,512]{1,0:T(8,128)(2,1)}, f32[32,128]{1,0:T(8,128)}) custom-call(s32[8,2048]{1,0:T(8,128)} %bitcast.8, f32[8,2048]{1,0:T(8,128)} %get-tuple-element.18.pre_ref, f32[8,2048]{1,0:T(8,128)} %get-tuple-element.19.back_ref, bf16[4096,128]{1,0:T(8,128)(2,1)} %get-tuple-element.20.base_ref, ...), custom_call_target="tpu_custom_call" | custom-call | tf_op jit(solution)/shard_map/grads/pallas_call | solution.py:614
  135.4 0.0 copy-done.1
  135.4 0.7 copy.17
  136.1 0.0 copy-done.2
  136.1 0.6 copy.18
  136.7 0.0 copy-done
  136.7 0.7 copy.19
Async XLA Ops:
  102.0 33.4 %copy-start.1 = (bf16[128,512]{1,0:T(8,128)(2,1)S(1)}, bf16[128,512]{1,0:T(8,128)(2,1)}, u32[]{:S(2)}) copy-start(bf16[128,512]{1,0:T(8,128)(2,1)} %get-tuple-element.34) | copy-start | bytes 393220
  102.0 34.0 %copy-start.2 = (f32[1,512]{1,0:T(1,128)S(1)}, f32[1,512]{1,0:T(1,128)}, u32[]{:S(2)}) copy-start(f32[1,512]{1,0:T(1,128)} %get-tuple-element.26) | copy-start | bytes 6148
  102.0 34.6 %copy-start = (bf16[256,512]{1,0:T(8,128)(2,1)S(1)}, bf16[256,512]{1,0:T(8,128)(2,1)}, u32[]{:S(2)}) copy-start(bf16[256,512]{1,0:T(8,128)(2,1)} %get-tuple-element.39) | copy-start | bytes 786436

commit v6 on v5

--- a/solution.py
+++ b/solution.py
@@ -114,40 +114,46 @@
 
 def pick_slots(rows, w_ref, ids, bias):
     width = 256
-    accs = [jnp.zeros((8, PAIR), F32) for _ in range(SLOTS)]
+    accs = [[jnp.zeros((8, 128), F32)] * SLOTS for _ in range(2)]
     for c in range(FEATS // width):
         lines = slice(c * width, (c + 1) * width)
         dots = lax.dot_general(
             w_ref[lines, :], rows, (((1,), (1,)), ((), ())), preferred_element_type=F32
         )
-        if bias is not None:
-            dots = dots + jnp.concatenate([bias[lines, :]] * 2, axis=1)
-        for j in range(SLOTS):
-            row = ids[j : j + 1, :]
-
-            def narrow(tree, down_to):
-                while tree.shape[0] > down_to:
-                    half = tree.shape[0] // 2
-                    upper = jnp.broadcast_to((row & half) != 0, (half, PAIR))
-                    tree = jnp.where(upper, tree[half:], tree[:half])
-                return tree
-
-            blocks = [narrow(dots[64 * i : 64 * (i + 1)], 8) for i in range(width // 64)]
-            tree = blocks
-            bit = 64
-            while len(tree) > 1:
-                upper = jnp.broadcast_to((row & bit) != 0, (8, PAIR))
-                tree = [jnp.where(upper, b, a) for a, b in zip(tree[::2], tree[1::2])]
-                bit *= 2
-            tree = tree[0]
-            here = jnp.broadcast_to((row >> 8) == c, (8, PAIR))
-            accs[j] = jnp.where(here, tree, accs[j])
-    line = lax.broadcasted_iota(jnp.int32, (8, PAIR), 0)
+        for t in range(2):
+            part = dots[:, t * 128 : (t + 1) * 128]
+            if bias is not None:
+                part = part + bias[lines, :]
+            accs[t] = [
+                pick_row(part, ids[j : j + 1, t * 128 : (t + 1) * 128], c, accs[t][j])
+                for j in range(SLOTS)
+            ]
+    line = lax.broadcasted_iota(jnp.int32, (8, 128), 0)
     out = []
     for j in range(SLOTS):
-        hit = line == (ids[j : j + 1, :] & 7)
-        out.append(jnp.sum(jnp.where(hit, accs[j], 0.0), axis=0, keepdims=True))
+        both = []
+        for t in range(2):
+            hit = line == (ids[j : j + 1, t * 128 : (t + 1) * 128] & 7)
+            both.append(jnp.sum(jnp.where(hit, accs[t][j], 0.0), axis=0, keepdims=True))
+        out.append(jnp.concatenate(both, axis=1))
     return jnp.concatenate(out, axis=0)
+
+
+def pick_row(dots, row, c, acc):
+    def narrow(tree):
+        while tree.shape[0] > 8:
+            half = tree.shape[0] // 2
+            upper = jnp.broadcast_to((row & half) != 0, (half, 128))
+            tree = jnp.where(upper, tree[half:], tree[:half])
+        return tree
+
+    tree = [narrow(dots[64 * i : 64 * (i + 1)]) for i in range(dots.shape[0] // 64)]
+    bit = 64
+    while len(tree) > 1:
+        upper = jnp.broadcast_to((row & bit) != 0, (8, 128))
+        tree = [jnp.where(upper, b, a) for a, b in zip(tree[::2], tree[1::2])]
+        bit *= 2
+    return jnp.where(jnp.broadcast_to((row >> 8) == c, (8, 128)), tree[0], acc)
 
 
 def gather_and_pick(at, net, pnet, own, rows_ref, w_ref, id_ref, bias, parts, keep, extra):
@@ -571,13 +577,17 @@
 
 
 def grad_kernel(
-    id_ref, pre_ref, back_ref, base_ref, x_ref, r_ref, ge_ref, gd_ref, gb_ref, st_ref, at_ref
+    id_ref, pre_ref, back_ref, base_ref, x_ref, r_ref, c_in, gs_in, bd_in,
+    ge_ref, gd_ref, gb_ref, c_ref, gs_ref, bd_ref, st_ref, at_ref
 ):
     feats = base_ref.shape[0]
 
     @pl.when(pl.program_id(0) == 0)
     def _():
         gb_ref[...] = bias_grads(id_ref, pre_ref, back_ref)
+        c_ref[...] = c_in[...]
+        gs_ref[...] = gs_in[...]
+        bd_ref[...] = bd_in[...]
 
     for t in range(TOKENS // 128):
         lanes = slice(t * 128, (t + 1) * 128)
@@ -607,21 +617,24 @@
     gd_ref[...] = jnp.dot(at_ref[...], r_ref[...], preferred_element_type=F32).astype(BF16)
 
 
-def grads(ids, pre, back, base, x, r, feats=1024):
+def grads(ids, pre, back, base, x, r, recon, grad_skip, grad_bdec, feats=1024):
     slots = pl.BlockSpec((SLOTS, TOKENS), lambda i: (0, 0))
     whole = pl.BlockSpec((TOKENS, COLS), lambda i: (0, 0))
     out = pl.BlockSpec((feats, COLS), lambda i: (i, 0))
+    small = [pl.BlockSpec(v.shape, lambda i: (0, 0)) for v in (recon, grad_skip, grad_bdec)]
     return pl.pallas_call(
         grad_kernel,
         grid=(FEATS // feats,),
-        in_specs=[slots, slots, slots, pl.BlockSpec((feats, 128), lambda i: (i, 0)), whole, whole],
-        out_specs=[out, out, pl.BlockSpec((FEATS // 128, 128), lambda i: (0, 0))],
+        in_specs=[slots, slots, slots, pl.BlockSpec((feats, 128), lambda i: (i, 0)), whole, whole]
+        + small,
+        out_specs=[out, out, pl.BlockSpec((FEATS // 128, 128), lambda i: (0, 0))] + small,
         out_shape=[jax.ShapeDtypeStruct((FEATS, COLS), BF16)] * 2
-        + [jax.ShapeDtypeStruct((FEATS // 128, 128), F32)],
+        + [jax.ShapeDtypeStruct((FEATS // 128, 128), F32)]
+        + [jax.ShapeDtypeStruct(v.shape, v.dtype) for v in (recon, grad_skip, grad_bdec)],
         scratch_shapes=[pltpu.VMEM((feats, TOKENS), BF16)] * 2,
         compiler_params=pltpu.CompilerParams(vmem_limit_bytes=VMEM_LIMIT),
         name="grads",
-    )(ids, pre, back, base, x, r)
+    )(ids, pre, back, base, x, r, recon, grad_skip, grad_bdec)
 
 
 def bias_grads(id_ref, pre_ref, back_ref):
@@ -649,7 +662,9 @@
     recon, all_x, all_r, pre, back, base, grad_skip, grad_bdec = step(
         inputs, ids, w_enc, b_enc.reshape(FEATS // 128, 128), w_dec, w_skip, target, b_dec[None, :]
     )
-    grad_enc, grad_dec, grad_benc = grads(ids, pre, back, base, all_x, all_r)
+    grad_enc, grad_dec, grad_benc, recon, grad_skip, grad_bdec = grads(
+        ids, pre, back, base, all_x, all_r, recon, grad_skip, grad_bdec
+    )
     return recon, grad_enc, grad_dec, grad_benc.reshape(-1), grad_bdec.reshape(-1), grad_skip
 
 

time: 137 us -> 136 us (level)
  local copies, waits for them, and re-layouts: 1.95 us -> 0 us
    unnamed x9 -> x0, local copies, waits for them, and re-layouts: 1.95 us -> none
where the time goes in v6:
time: 136 us; the launch traced here: 135 us
  Pallas kernels  135 us (99%)
    pallas_call x1, Pallas kernels, step(): pl.pallas_call(step_kernel, out_shape=[jax.ShapeDtypeStruct((ROWS, COLS),...  101 us
    pallas_call x1, Pallas kernels, grads(): pl.pallas_call(grad_kernel, grid=(FEATS // feats,), in_specs=[slots, slot...  33.4 us

profile of v6, /device:TPU:0, one launch (start us, length us, event | category | flops | bytes accessed | tf_op | source)
XLA Modules:
  0.0 135.4 jit_solution(9609588915522506559)
XLA Ops:
  0.6 101.4 %step.1 = (bf16[128,512]{1,0:T(8,128)(2,1)}, bf16[2048,512]{1,0:T(8,128)(2,1)}, bf16[2048,512]{1,0:T(8,128)(2,1)}, f32[8,2048]{1,0:T(8,128)}, f32[8,2048]{1,0:T(...) custom-call(bf16[128,512]{1,0:T(8,128)(2,1)} %x_ref.1, s32[8,2048]{1,0:T(8,128)} %bitcast.7, ...), custom_call_target="tpu_custom_call" | custom-call | tf_op jit(solution)/shard_map/step/pallas_call | solution.py:533
  102.0 33.4 %grads.1 = (bf16[4096,512]{1,0:T(8,128)(2,1)}, bf16[4096,512]{1,0:T(8,128)(2,1)}, f32[32,128]{1,0:T(8,128)}, bf16[128,512]{1,0:T(8,128)(2,1)}, bf16[256,512]{1,0:T(8,128)(2,1)}, /*index=5*/f32[1,512]{1,0:T(1,128)}) custom-call(s32[8,2048]{1,0:T(8,128)} %bitcast.8, f32[8,2048]{1,0:T(8,128)} %get-tuple-element.20.pre_ref, ...), custom_call_target="tpu_custom_call" | custom-call | tf_op jit(solution)/shard_map/grads/pallas_call | solution.py:625

commit v7 on v6

--- a/solution.py
+++ b/solution.py
@@ -426,7 +426,7 @@
         if i == 4:
             downward(0)
         if i == 6:
-            far_out[...] = here_sum(0)
+            far_out[...] = here_sum(0).astype(BF16)
             ynet.start(8, far_out, far_in, at.far)
             upward(1)
         if i == 7:
@@ -481,7 +481,7 @@
     lax.fori_loop(0, 8, body, 0)
     total = here_sum(1) + dec_bias[...]
     ynet.wait(8, far_in)
-    total = total + far_in[...]
+    total = total + far_in[...].astype(F32)
     recon[...] = total.astype(BF16)
     res[...] = (total - target[...].astype(F32)).astype(BF16)
     own = pltpu.make_async_copy(res, res_ref.at[seq_rows(at.s)], local.at[6])
@@ -562,8 +562,8 @@
             pltpu.VMEM((6, ROWS, COLS), BF16),
             pltpu.VMEM((4, ROWS // 2, COLS), BF16),
             pltpu.VMEM((4, ROWS, COLS), BF16),
-            pltpu.VMEM((ROWS, COLS), F32),
-            pltpu.VMEM((ROWS, COLS), F32),
+            pltpu.VMEM((ROWS, COLS), BF16),
+            pltpu.VMEM((ROWS, COLS), BF16),
             pltpu.VMEM((ROWS, COLS), BF16),
             dma((SEQ_KINDS,)), dma((SEQ_KINDS,)), dma((8, N_TP)), dma((8, N_TP)),
             dma((11,)), dma((11,)), dma((8,)), dma((8,)), dma((9,)), dma((9,)),

time: 136 us -> 136 us (level)
  no operation moved by 1% of the time
where the time goes in v7:
time: 136 us; the launch traced here: 135 us
  Pallas kernels  135 us (99%)
    pallas_call x1, Pallas kernels, step(): pl.pallas_call(step_kernel, out_shape=[jax.ShapeDtypeStruct((ROWS, COLS),...  101 us
    pallas_call x1, Pallas kernels, grads(): pl.pallas_call(grad_kernel, grid=(FEATS // feats,), in_specs=[slots, slot...  33.4 us

profile of v7, /device:TPU:0, one launch (start us, length us, event | category | flops | bytes accessed | tf_op | source)
XLA Modules:
  0.0 135.4 jit_solution(3030409275964551673)
XLA Ops:
  0.6 101.4 %step.1 = (bf16[128,512]{1,0:T(8,128)(2,1)}, bf16[2048,512]{1,0:T(8,128)(2,1)}, bf16[2048,512]{1,0:T(8,128)(2,1)}, f32[8,2048]{1,0:T(8,128)}, f32[8,2048]{1,0:T(...) custom-call(bf16[128,512]{1,0:T(8,128)(2,1)} %x_ref.1, s32[8,2048]{1,0:T(8,128)} %bitcast.7, ...), custom_call_target="tpu_custom_call" | custom-call | tf_op jit(solution)/shard_map/step/pallas_call | solution.py:533
  102.0 33.4 %grads.1 = (bf16[4096,512]{1,0:T(8,128)(2,1)}, bf16[4096,512]{1,0:T(8,128)(2,1)}, f32[32,128]{1,0:T(8,128)}, bf16[128,512]{1,0:T(8,128)(2,1)}, bf16[256,512]{1,0:T(8,128)(2,1)}, /*index=5*/f32[1,512]{1,0:T(1,128)}) custom-call(s32[8,2048]{1,0:T(8,128)} %bitcast.8, f32[8,2048]{1,0:T(8,128)} %get-tuple-element.20.pre_ref, ...), custom_call_target="tpu_custom_call" | custom-call | tf_op jit(solution)/shard_map/grads/pallas_call | solution.py:625
